TPU v7x, 512 devices: a whole 4x8x8 slice. The times are simulated.
512 devices in a mesh: expert: 128 (over z_hi, x, y), dp: 4 (over z_lo, core).
Axes of the slice: x: 4, y: 8, z: 8 (z_hi: 4, z_lo: 2; z = z_hi * 2 + z_lo), core: 2. Of those that a mesh axis runs over, the one named last changes fastest.
Arguments:
- tokens: bfloat16 [512, 128, 1280], P(('expert', 'dp')), may hold values from -26 to 26
- grad_out: bfloat16 [512, 128, 1280], P(('expert', 'dp')), may hold values from -6 to 6
- router: bfloat16 [1280, 64], replicated, may hold values from -26 to 26
- up_weight: bfloat16 [128, 1280, 1536], P('expert', None, 'dp'), may hold values from -0.15625 to 0.15625
- down_weight: bfloat16 [128, 1280, 1536], P('expert', None, 'dp'), may hold values from -0.109375 to 0.109375
Outputs:
- grad_tokens: bfloat16 [512, 128, 1280], P(('expert', 'dp'))
- grad_router: float32 [1280, 64], P('dp')
- grad_up: bfloat16 [128, 1280, 1536], P('expert', None, 'dp')
- grad_down: bfloat16 [128, 1280, 1536], P('expert', None, 'dp')
All inputs are finite; a program needn't handle non-finite values.
Results may differ from a plain program's by a relative error of at most 0.035.
Values may be sent and summed in bfloat16 or wider, within the bound.
A program may use at most 64 MiB of HBM per device.

v0:
```python
import jax
import jax.numpy as jnp
from jax import lax
from jax.sharding import PartitionSpec as P

logit_scale = 24.0


def exact_gelu(value):
    return jax.nn.gelu(value, approximate=False)


def front(image, router32):
    xf = image.astype(jnp.float32)
    x_norm = xf * lax.rsqrt(jnp.sum(xf * xf, axis=1, keepdims=True) + 1e-06)
    r_norm = router32 * lax.rsqrt(jnp.sum(router32 * router32, axis=0, keepdims=True) + 1e-06)
    logits = logit_scale * jnp.dot(x_norm, r_norm, precision=lax.Precision.HIGHEST)
    weights = jnp.exp(logits)
    dispatch = (weights / jnp.sum(weights, axis=0, keepdims=True)).astype(jnp.bfloat16)
    combine = (weights / jnp.sum(weights, axis=1, keepdims=True)).astype(jnp.bfloat16)
    slots_in = jnp.dot(dispatch.T, image, preferred_element_type=jnp.float32).astype(jnp.bfloat16)
    return (slots_in, combine)


def rounded(value):
    return lax.optimization_barrier(value.astype(jnp.bfloat16)).astype(jnp.float32)


def times_rows(left, weight):
    return lax.dot_general(
        left, weight, (((1,), (1,)), ((), ())), preferred_element_type=jnp.float32
    )


def local(tokens, grad_out, router, up_weight, down_weight):
    image = tokens[0]
    slots_in, front_back = jax.vjp(front, image, router.astype(jnp.float32))
    slot_rows, combine = slots_in
    own_rows = slot_rows.shape[0] * 2
    sent = jnp.repeat(slot_rows, 2, axis=0)
    received = lax.all_to_all(sent, "expert", split_axis=0, concat_axis=0, tiled=True)
    w_up = up_weight[0]
    w_down = down_weight[0]
    n_dp = lax.axis_size("dp")
    full_up, full_down = (
        lax.all_gather(w_up, "dp", axis=1, tiled=True),
        lax.all_gather(w_down, "dp", axis=1, tiled=True),
    )
    own_act = exact_gelu(jnp.dot(received, full_up, preferred_element_type=jnp.float32)).astype(
        jnp.bfloat16
    )
    piece = w_up.shape[1]
    parts = jnp.einsum(
        "rpk,dpk->prd",
        own_act.reshape(own_rows, n_dp, piece),
        full_down.reshape(full_down.shape[0], n_dp, piece),
        preferred_element_type=jnp.float32,
    )
    half_sum = jnp.sum(rounded(parts), axis=0)
    rows = lax.all_gather(received, "dp", axis=0, tiled=True)
    pre = jnp.dot(rows, w_up, preferred_element_type=jnp.float32)
    act = exact_gelu(pre).astype(jnp.bfloat16)
    returned = lax.all_to_all(
        half_sum.astype(jnp.bfloat16), "expert", split_axis=0, concat_axis=0, tiled=True
    ).astype(half_sum.dtype)
    slots_out = jnp.sum(returned.reshape(own_rows // 2, 2, returned.shape[1]), axis=1).astype(
        jnp.bfloat16
    )
    cotangent = grad_out[0]
    grad_combine = lax.dot_general(
        cotangent, slots_out, (((1,), (1,)), ((), ())), preferred_element_type=jnp.float32
    ).astype(jnp.bfloat16)
    grad_slots_out = lax.dot_general(
        combine, cotangent, (((0,), (0,)), ((), ())), preferred_element_type=jnp.float32
    ).astype(jnp.bfloat16)
    grad_sent = jnp.repeat(grad_slots_out, 2, axis=0)
    grad_received = lax.all_to_all(grad_sent, "expert", split_axis=0, concat_axis=0, tiled=True)
    grad_rows = lax.all_gather(grad_received, "dp", axis=0, tiled=True)
    grad_act = jnp.dot(grad_rows, w_down, preferred_element_type=jnp.float32)
    gelu_back = jax.vjp(exact_gelu, pre)[1]
    grad_pre = gelu_back(grad_act)[0].astype(jnp.bfloat16)
    grad_down_piece = lax.dot_general(
        grad_rows, act, (((0,), (0,)), ((), ())), preferred_element_type=jnp.float32
    ).astype(jnp.bfloat16)
    grad_up_piece = lax.dot_general(
        rows, grad_pre, (((0,), (0,)), ((), ())), preferred_element_type=jnp.float32
    ).astype(jnp.bfloat16)
    half_grad = lax.psum_scatter(
        rounded(times_rows(grad_pre, w_up)).astype(jnp.bfloat16),
        "dp",
        scatter_dimension=0,
        tiled=True,
    ).astype(jnp.float32)
    grad_returned = lax.all_to_all(
        half_grad.astype(jnp.bfloat16), "expert", split_axis=0, concat_axis=0, tiled=True
    ).astype(half_grad.dtype)
    grad_slots_in = jnp.sum(
        grad_returned.reshape(own_rows // 2, 2, grad_returned.shape[1]), axis=1
    ).astype(jnp.bfloat16)
    grad_image, router_term = front_back((grad_slots_in, grad_combine))
    router_whole = lax.psum(router_term, "expert")
    router_grad = lax.psum_scatter(
        router_whole.astype(jnp.bfloat16), "dp", scatter_dimension=0, tiled=True
    ).astype(jnp.float32)
    return (grad_image[None], router_grad, grad_up_piece[None], grad_down_piece[None])


def solution(mesh):
    placed = (
        P(("expert", "dp"), None, None),
        P(("expert", "dp"), None, None),
        P(),
        P("expert", None, "dp"),
        P("expert", None, "dp"),
    )
    return jax.shard_map(
        local,
        mesh=mesh,
        in_specs=placed,
        out_specs=(
            P(("expert", "dp"), None, None),
            P("dp", None),
            P("expert", None, "dp"),
            P("expert", None, "dp"),
        ),
        check_vma=False,
    )
```

profile of v0, /device:TPU:1, one launch (start us, length us, event | category | flops | bytes accessed | tf_op | source)
XLA Modules:
  0.0 1069.6 jit_solution(1168587797215216612)
XLA Ops:
  7.2 1.1 fusion.48
  8.3 1.1 fusion.42
  9.5 2.0 fusion.67
  11.5 1.2 convolution_convert_fusion.6
  13.7 2.7 reduce.6
  16.5 36.4 %all_to_all.50 = bf16[128,2,640]{2,1,0:T(2,128)(2,1)S(1)} all-to-all(bf16[128,2,640]{2,1,0:T(2,128)(2,1)S(1)} %reshape.91), channel_id=1, replica_groups=mesh['expert'=128,'dp'=4] {'expert'}, dimensions={0} | all-to-all | bytes 655360 | tf_op jit(solution)/shard_map/all_to_all | solution.py:41
  54.7 2.7 reduce.5
  57.4 22.7 %all_to_all.51 = bf16[128,2,640]{2,1,0:T(2,128)(2,1)S(1)} all-to-all(bf16[128,2,640]{2,1,0:T(2,128)(2,1)S(1)} %reshape.89), channel_id=1, replica_groups=mesh['expert'=128,'dp'=4] {'expert'}, dimensions={0} | all-to-all | bytes 655360 | tf_op jit(solution)/shard_map/all_to_all | solution.py:77
  81.4 2.1 all-gather.9.cloned.1.call-done
  83.6 2.2 fusion.10
  85.7 29.2 %all-gather.11.cloned.1.call-done = bf16[512,1,1280]{2,0,1:T(8,128)(2,1)} async-done(((bf16[128,1,1280]{2,0,1:T(8,128)(2,1)}), bf16[512,1,1280]{2,0,1:T(8,128)(2,1)}) %all-gather.11.cloned.1.call-update) | async-done | bytes 1310736 | tf_op jit(solution)/shard_map/all_gather | solution.py:78
  115.0 3.8 add_convert_fusion
  118.8 1.9 convolution_convert_fusion
  121.4 1.3 copy.22
  122.7 25.7 %reduce-scatter.5.cloned.1.call-done = bf16[128,1280]{1,0:T(8,128)(2,1)} async-done(((bf16[512,1280]{1,0:T(8,128)(2,1)}), bf16[128,1280]{1,0:T(8,128)(2,1)}) %reduce-scatter.5.cloned.1.call-update) | async-done | bytes 327696 | tf_op jit(solution)/shard_map/reduce_scatter | solution.py:88
  148.4 1.8 reduce.7
  151.0 16.0 %all-to-all-start.2 = ((bf16[128,2,640]{2,1,0:T(2,128)(2,1)}), bf16[128,2,640]{2,1,0:T(2,128)(2,1)S(1)}, u32[]{:S(2)}, u32[]{:S(2)}) async-start(bf16[128,2,640]{2,1,0:T(2,128)(2,1)} %reshape.93), calls=%async_computation.3 | async-start | bytes 655360 | tf_op jit(solution)/shard_map/all_to_all | solution.py:94
  167.0 40.7 %all-gather.13.cloned.1.call-done = bf16[1,1280,1536]{2,1,0:T(8,128)(2,1)} async-done(((bf16[1,1280,384]{2,1,0:T(8,128)(2,1)}), bf16[1,1280,1536]{2,1,0:T(8,128)(2,1)}) %all-gather.13.cloned.1.call-update) | async-done | bytes 3932176 | tf_op jit(solution)/shard_map/all_gather | solution.py:46
  207.7 4.3 fusion.21
  212.0 48.1 %all-gather.15.cloned.1.call-done = bf16[1,1280,1536]{1,2,0:T(8,128)(2,1)} async-done(((bf16[1,1280,384]{1,2,0:T(8,128)(2,1)}), bf16[1,1280,1536]{1,2,0:T(8,128)(2,1)}) %all-gather.15.cloned.1.call-update) | async-done | bytes 3932176 | tf_op jit(solution)/shard_map/all_gather | solution.py:47
  260.1 3.0 convolution_convert_fusion.1
  263.3 0.9 reduce.8
  265.0 15.7 %all-to-all-start.3 = ((bf16[128,2,640]{2,1,0:T(2,128)(2,1)}), bf16[128,2,640]{2,1,0:T(2,128)(2,1)S(1)}, u32[]{:S(2)}, u32[]{:S(2)}) async-start(bf16[128,2,640]{2,1,0:T(2,128)(2,1)} %reshape.95), calls=%async_computation.4 | async-start | bytes 655360 | tf_op jit(solution)/shard_map/all_to_all | solution.py:63
  281.0 4.6 fusion.3
  285.7 1.8 fusion.2
  287.8 2.0 reduce.3
  291.0 6.9 all-to-all-done.3
  298.1 2.0 reduce.4
  303.2 631.7 %all-reduce.1 = bf16[1280,64]{0,1:T(8,128)(2,1)S(1)} all-reduce(f32[1280,64]{0,1:T(8,128)S(1)} %add_add_fusion.1), channel_id=1, replica_groups=mesh['expert'=128,'dp'=4] {'expert'}, use_global_device_ids=true, to_apply=%region_12.0 | all-reduce | flops 81920 | bytes 491520 | tf_op jit(solution)/shard_map/psum | solution.py:101
  935.7 1.1 fusion.5
  936.8 124.2 %reduce-scatter.7.cloned.1.call-done = bf16[320,64]{1,0:T(8,128)(2,1)} async-done(((bf16[1280,64]{1,0:T(8,128)(2,1)}), bf16[320,64]{1,0:T(8,128)(2,1)}) %reduce-scatter.7.cloned.1.call-update) | async-done | bytes 40976
  1061.1 1.0 copy.28
  (67 shorter events, 13.3 us)
Async XLA Ops:
  7.2 46.8 %copy-start = (bf16[1,128,1280]{2,1,0:T(8,128)(2,1)S(1)}, bf16[1,128,1280]{2,1,0:T(8,128)(2,1)}, u32[]{:S(2)}) copy-start(bf16[1,128,1280]{2,1,0:T(8,128)(2,1)} %param.6) | copy-start | bytes 983044
  7.2 76.4 %all-gather.9.cloned.1.call-start = ((), (), s32[]{:S(2)}) async-start(), calls=%async_computation.7 | async-start | bytes 1638400 | tf_op jit(solution)/shard_map/all_gather | solution.py:60
  53.9 61.0 %all-gather.11.cloned.1.call-start = ((), (), s32[]{:S(2)}) async-start(), calls=%async_computation.8 | async-start | bytes 1638400 | tf_op jit(solution)/shard_map/all_gather | solution.py:78
  80.1 3.5 copy-start.2
  81.2 33.8 %copy-start.5 = (bf16[1,1280,384]{2,1,0:T(8,128)(2,1)S(1)}, bf16[1,1280,384]{2,1,0:T(8,128)(2,1)}, u32[]{:S(2)}) copy-start(bf16[1,1280,384]{2,1,0:T(8,128)(2,1)} %param.9) | copy-start | bytes 2949124
  81.2 67.2 %reduce-scatter.5.cloned.1.call-start = ((), (), s32[]{:S(2)}) async-start(), calls=%async_computation.6 | async-start | bytes 1638400 | tf_op jit(solution)/shard_map/reduce_scatter | solution.py:88
  85.7 33.0 %copy-start.7 = (f32[512,384]{1,0:T(8,128)}, f32[512,384]{1,0:T(8,128)S(1)}, u32[]{:S(2)}) copy-start(f32[512,384]{1,0:T(8,128)S(1)} %fusion.10) | copy-start | bytes 2359300
  120.7 87.0 %all-gather.13.cloned.1.call-start = ((), (), s32[]{:S(2)}) async-start(), calls=%async_computation.9 | async-start | bytes 4915200 | tf_op jit(solution)/shard_map/all_gather | solution.py:46
  121.3 138.8 %all-gather.15.cloned.1.call-start = ((), (), s32[]{:S(2)}) async-start(), calls=%async_computation.10 | async-start | bytes 4915200 | tf_op jit(solution)/shard_map/all_gather | solution.py:47
  122.7 85.0 %copy-start.4 = (bf16[128,1,1280]{2,0,1:T(8,128)(2,1)S(1)}, bf16[128,1,1280]{2,0,1:T(8,128)(2,1)}, u32[]{:S(2)}) copy-start(bf16[128,1,1280]{2,0,1:T(8,128)(2,1)} %copy.18) | copy-start | bytes 983044
  151.0 113.9 %all-to-all-start.2 = ((bf16[128,2,640]{2,1,0:T(2,128)(2,1)}), bf16[128,2,640]{2,1,0:T(2,128)(2,1)S(1)}, u32[]{:S(2)}, u32[]{:S(2)}) async-start(bf16[128,2,640]{2,1,0:T(2,128)(2,1)} %reshape.93), calls=%async_computation.3 | async-start | bytes 655360 | tf_op jit(solution)/shard_map/all_to_all | solution.py:94
  263.3 17.8 %copy-start.8 = (f32[512,384]{1,0:T(8,128)S(1)}, f32[512,384]{1,0:T(8,128)}, u32[]{:S(2)}) copy-start(f32[512,384]{1,0:T(8,128)} %copy-done.7) | copy-start | bytes 2359300
  265.0 32.8 %all-to-all-start.3 = ((bf16[128,2,640]{2,1,0:T(2,128)(2,1)}), bf16[128,2,640]{2,1,0:T(2,128)(2,1)S(1)}, u32[]{:S(2)}, u32[]{:S(2)}) async-start(bf16[128,2,640]{2,1,0:T(2,128)(2,1)} %reshape.95), calls=%async_computation.4 | async-start | bytes 655360 | tf_op jit(solution)/shard_map/all_to_all | solution.py:63
  280.7 4.9 copy-start.6
  280.7 780.3 %reduce-scatter.7.cloned.1.call-start = ((), (), s32[]{:S(2)}) async-start(), calls=%async_computation.11 | async-start | bytes 409600
  287.8 3.0 copy-start.1
  298.1 3.3 copy-start.3
Sparse Core Ops, SparseCore 0:
  54.1 29.4 all-gather.8
  86.2 28.7 all-gather.10
  120.9 27.5 reduce-scatter.4
  150.4 57.2 all-gather.12
  210.2 49.8 all-gather.14
  935.8 125.1 reduce-scatter.6
where the time goes:
time: 1070 us
  blocking collectives  691 us (65%)
  waiting for transfers between devices  278 us (26%)
  starting transfers between devices  32.4 us (3%)
  matrix products  28.2 us (3%)
  other arithmetic  17 us (2%)
  between operations  14.5 us (1%)
    psum x1, blocking collectives, local(): router_whole = lax.psum(router_term, 'expert')  632 us
    unnamed x7, waiting for transfers between devices  125 us
    all_gather x1, waiting for transfers between devices, local(): lax.all_gather(w_down, 'dp', axis=1, tiled=True)  48.1 us
    all_gather x1, waiting for transfers between devices, local(): lax.all_gather(w_up, 'dp', axis=1, tiled=True)  40.7 us
    all_to_all x1, blocking collectives, local(): lax.all_to_all(sent, 'expert', split_axis=0, concat_axis=0, tiled=True)  36.4 us
    all_gather x1, waiting for transfers between devices, local(): grad_rows = lax.all_gather(grad_received, 'dp', axis=0, tiled=True)  29.2 us
    reduce_scatter x1, waiting for transfers between devices, local(): lax.psum_scatter(rounded(times_rows(grad_pre, w_up)).astype(jnp.bfloat16)...  25.7 us
    all_to_all x1, blocking collectives, local(): lax.all_to_all(grad_sent, 'expert', split_axis=0, concat_axis=0, tiled=True)  22.7 us
  transfers between devices with their start and end apart: 8, of which 7 were waited for; matrix products, arithmetic and copies ran while one was open for 3% of the time, Pallas kernels for 0%

commit v1 on v0

v1 whole, which is shorter than its diff:
```python
import jax
import jax.numpy as jnp
from jax import lax
from jax.sharding import PartitionSpec as P

logit_scale = 24.0
f32 = jnp.float32
bf16 = jnp.bfloat16


def exact_gelu(value):
    return jax.nn.gelu(value, approximate=False)


def dot(a, b, ca, cb):
    return lax.dot_general(a, b, (((ca,), (cb,)), ((), ())), preferred_element_type=f32)


def front(x, go, rt):
    xf = x.astype(f32)
    rf = rt.astype(f32)
    inv_x = lax.rsqrt(jnp.sum(xf * xf, axis=1, keepdims=True) + 1e-06)
    inv_r = lax.rsqrt(jnp.sum(rf * rf, axis=1, keepdims=True) + 1e-06).T
    logits = (logit_scale * inv_x) * inv_r * dot(x, rt, 1, 1)
    e = jnp.exp(logits)
    disp = e / jnp.sum(e, axis=0, keepdims=True)
    comb = e / jnp.sum(e, axis=1, keepdims=True)
    slots = dot(disp.astype(bf16), x, 0, 0).astype(bf16)
    grads = dot(comb.astype(bf16), go, 0, 0).astype(bf16)
    return inv_x, inv_r, logits, disp, comb, slots, grads


def back(x, go, rt, saved, slots_out, grad_slots):
    inv_x, inv_r, logits, disp, comb = saved
    d_comb = dot(go, slots_out, 1, 1).astype(bf16).astype(f32)
    d_disp = dot(x, grad_slots, 1, 1).astype(bf16).astype(f32)
    d_log = disp * (d_disp - jnp.sum(disp * d_disp, axis=0, keepdims=True)) + comb * (
        d_comb - jnp.sum(comb * d_comb, axis=1, keepdims=True)
    )
    m = d_log * logits
    row = jnp.sum(m, axis=1, keepdims=True)
    col = jnp.sum(m, axis=0, keepdims=True)
    a = (logit_scale * inv_x) * inv_r * d_log
    hi = a.astype(bf16)
    lo = (a - hi.astype(f32)).astype(bf16)
    left = jnp.concatenate([disp.astype(bf16), hi, lo], axis=1)
    right = jnp.concatenate([grad_slots, rt, rt], axis=0)
    grad_x = dot(left, right, 1, 0) - x.astype(f32) * (inv_x * inv_x * row)
    term = dot(jnp.concatenate([hi, lo], axis=1), x, 0, 0)
    term = term[:64] + term[64:] - rt.astype(f32) * (inv_r * inv_r * col).T
    return grad_x.astype(bf16), term


def local(tokens, grad_out, router, up_weight, down_weight):
    x, go, rt = tokens[0], grad_out[0], router.T
    w_up, w_down = up_weight[0], down_weight[0]
    *saved, slots, grads = front(x, go, rt)
    both = jnp.stack([slots, grads], axis=1)
    sent = jnp.repeat(both, 2, axis=0)
    got = lax.all_to_all(sent, "expert", split_axis=0, concat_axis=0, tiled=True)
    rows = lax.all_gather(got[:, 0], "dp", axis=0, tiled=True)
    grows = lax.all_gather(got[:, 1], "dp", axis=0, tiled=True)
    pre = dot(rows, w_up, 1, 0)
    act, gelu_back = jax.vjp(exact_gelu, pre)
    act = act.astype(bf16)
    grad_act = dot(grows, w_down, 1, 0)
    grad_pre = gelu_back(grad_act)[0].astype(bf16)
    part_y = dot(act, w_down, 1, 1).astype(bf16)
    part_x = dot(grad_pre, w_up, 1, 1).astype(bf16)
    y = lax.psum_scatter(part_y, "dp", scatter_dimension=0, tiled=True)
    dx = lax.psum_scatter(part_x, "dp", scatter_dimension=0, tiled=True)
    grad_down = dot(grows, act, 0, 0).astype(bf16)
    grad_up = dot(rows, grad_pre, 0, 0).astype(bf16)
    back_rows = lax.all_to_all(
        jnp.stack([y, dx], axis=1), "expert", split_axis=0, concat_axis=0, tiled=True
    )
    summed = jnp.sum(back_rows.reshape(64, 2, 2, -1).astype(f32), axis=1).astype(bf16)
    grad_x, term = back(x, go, rt, saved, summed[:, 0], summed[:, 1])
    n_dp, n_ex = lax.axis_size("dp"), lax.axis_size("expert")
    pieces = term.astype(bf16).reshape(64, n_dp, -1).transpose(1, 0, 2)
    pieces = pieces.reshape(n_dp, n_ex, -1)
    own = jnp.sum(lax.all_to_all(pieces, "dp", 0, 0, tiled=True).astype(f32), axis=0)
    own = lax.all_to_all(own.astype(bf16), "expert", 0, 0, tiled=True)
    own = jnp.sum(own.astype(f32), axis=0).astype(bf16)
    whole = lax.all_to_all(jnp.broadcast_to(own, (n_ex, own.shape[0])), "expert", 0, 0, tiled=True)
    router_grad = whole.reshape(64, -1).T.astype(f32)
    return (grad_x[None], router_grad, grad_up[None], grad_down[None])


def solution(mesh):
    placed = (
        P(("expert", "dp"), None, None),
        P(("expert", "dp"), None, None),
        P(),
        P("expert", None, "dp"),
        P("expert", None, "dp"),
    )
    return jax.shard_map(
        local,
        mesh=mesh,
        in_specs=placed,
        out_specs=(
            P(("expert", "dp"), None, None),
            P("dp", None),
            P("expert", None, "dp"),
            P("expert", None, "dp"),
        ),
        check_vma=False,
    )
```

time: 1070 us -> 279 us (0.26)
  blocking collectives: 691 us -> 82.1 us
  waiting for transfers between devices: 278 us -> 129 us
  starting transfers between devices: 32.4 us -> 18.9 us
  other arithmetic: 17 us -> 5.28 us
    psum x1 -> x0, blocking collectives: 632 us -> none  [local(): router_whole = lax.psum(router_term, 'expert')]
    unnamed x7 -> x4, waiting for transfers between devices: 125 us -> 0.07 us
    all_gather x4 -> x2, waiting for transfers between devices: 120 us -> 47.7 us  [the longest x1 25.9 us: local(): grows = lax.all_gather(got[:, 1], 'dp', axis=0, tiled=True)]
    reduce_scatter x1 -> x2, waiting for transfers between devices: 25.7 us -> 56.3 us  [the longest x1 30.7 us: local(): y = lax.psum_scatter(part_y, 'dp', scatter_dimension=0, tiled=True)]
    all_to_all x2 -> x3, waiting for transfers between devices: 6.87 us -> 24.7 us  [the longest x1 12.8 us: local(): own = lax.all_to_all(own.astype(bf16), 'expert', 0, 0, tiled=True)]
    all_to_all x1, blocking collectives: 22.7 us -> 38.8 us  [local(): lax.all_to_all(jnp.stack([y, dx], axis=1), 'expert', split_axis=0, concat...]
    all_to_all x2 -> x3, starting transfers between devices: 31.7 us -> 18.8 us  [the longest x1 6.83 us: local(): lax.all_to_all(jnp.broadcast_to(own, (n_ex, own.shape[0])), 'expert', 0,...]
    all_to_all x6 -> x0, other arithmetic: 12 us -> none  [the longest x2 3.75 us: local(): lax.all_to_all(half_grad.astype(jnp.bfloat16), 'expert', split_axis=0, co...]
  transfers between devices with their start and end apart: 8 -> 7, of which waited for: 7 -> 6; matrix products, arithmetic and copies ran while one was open for 3% -> 5% of each run, Pallas kernels for 0% -> 0%
where the time goes in v1:
time: 279 us; the launch traced here: 278 us
  waiting for transfers between devices  129 us (46%)
  blocking collectives  82.1 us (29%)
  matrix products  21.1 us (8%)
  starting transfers between devices  18.9 us (7%)
  between operations  14 us (5%)
  local copies, waits for them, and re-layouts  7.99 us (3%)
  other arithmetic  5.28 us (2%)
    all_to_all x1, blocking collectives, local(): lax.all_to_all(sent, 'expert', split_axis=0, concat_axis=0, tiled=True)  43.2 us
    all_to_all x1, blocking collectives, local(): lax.all_to_all(jnp.stack([y, dx], axis=1), 'expert', split_axis=0, concat...  38.8 us
    reduce_scatter x1, waiting for transfers between devices, local(): y = lax.psum_scatter(part_y, 'dp', scatter_dimension=0, tiled=True)  30.7 us
    all_gather x1, waiting for transfers between devices, local(): grows = lax.all_gather(got[:, 1], 'dp', axis=0, tiled=True)  25.9 us
    reduce_scatter x1, waiting for transfers between devices, local(): dx = lax.psum_scatter(part_x, 'dp', scatter_dimension=0, tiled=True)  25.7 us
    all_gather x1, waiting for transfers between devices, local(): rows = lax.all_gather(got[:, 0], 'dp', axis=0, tiled=True)  21.8 us
    dot_general x13, matrix products, dot(): lax.dot_general(a, b, (((ca,), (cb,)), ((), ())), preferred_element_type=...  21.1 us
    all_to_all x1, waiting for transfers between devices, local(): own = lax.all_to_all(own.astype(bf16), 'expert', 0, 0, tiled=True)  12.8 us
  transfers between devices with their start and end apart: 7, of which 6 were waited for; matrix products, arithmetic and copies ran while one was open for 5% of the time, Pallas kernels for 0%

profile of v1, /device:TPU:1, one launch (start us, length us, event | category | flops | bytes accessed | tf_op | source)
XLA Modules:
  0.0 278.2 jit_solution(12169025520208552819)
XLA Ops:
  7.2 1.2 fusion.36
  8.4 1.1 fusion.30
  9.6 1.4 exponential_reduce_fusion.1
  11.0 1.2 fusion.4
  13.1 43.2 %all_to_all.30 = bf16[128,2,1280]{2,1,0:T(2,128)(2,1)S(1)} all-to-all(bf16[128,2,1280]{2,1,0:T(2,128)(2,1)S(1)} %bitcast.88), channel_id=1, replica_groups=mesh['expert'=128,'dp'=4] {'expert'}, dimensions={0} | all-to-all | bytes 1310720 | tf_op jit(solution)/shard_map/all_to_all | solution.py:60
  56.4 0.9 fusion.62
  57.3 0.8 copy.41
  58.1 0.8 copy.42
  59.0 21.8 %all-gather.5.cloned.1.call-done = bf16[512,1,1280]{2,0,1:T(8,128)(2,1)} async-done(((bf16[128,1,1280]{2,0,1:T(8,128)(2,1)}), bf16[512,1,1280]{2,0,1:T(8,128)(2,1)}) %all-gather.5.cloned.1.call-update) | async-done | bytes 1310736 | tf_op jit(solution)/shard_map/all_gather | solution.py:61
  80.8 4.7 %multiply_convert_fusion = (bf16[512,384]{1,0:T(8,128)(2,1)S(1)}, f32[512,384]{1,0:T(8,128)}, f32[512,384]{1,0:T(8,128)}) fusion(bf16[1,1280,384]{2,1,0:T(8,128)(2,1)S(1)} %copy-done, bf16[512,1,1280]{2,0,1:T(8,128)(2,1)} %all-gather.5.cloned.1.call-done), kind=kOutput, calls=%fused_computation.35 | convolution fusion | flops 516096000 | bytes 4259840 | tf_op jit(solution)/shard_map/dot_general | solution.py:16
  85.5 25.9 %all-gather.7.cloned.1.call-done = bf16[512,1,1280]{2,0,1:T(8,128)(2,1)} async-done(((bf16[128,1,1280]{2,0,1:T(8,128)(2,1)}), bf16[512,1,1280]{2,0,1:T(8,128)(2,1)}) %all-gather.7.cloned.1.call-update) | async-done | bytes 1310736 | tf_op jit(solution)/shard_map/all_gather | solution.py:62
  111.4 2.8 %add_convert_fusion = bf16[512,384]{1,0:T(8,128)(2,1)S(1)} fusion(f32[512,384]{1,0:T(8,128)} %get-tuple-element.13, bf16[1,1280,384]{2,1,0:T(8,128)(2,1)S(1)} %copy-done.4, bf16[512,1,1280]{2,0,1:T(8,128)(2,1)} %all-gather.7.cloned.1.call-done, f32[512,384]{1,0:T(8,128)} %get-tuple-element.20), kind=kOutput, calls=%fused_computation.34 | convolution fusion | flops 506068992 | bytes 4259840 | tf_op jit(solution)/shard_map/dot_general | solution.py:16
  114.3 2.0 convolution_convert_fusion
  116.3 2.0 convolution_convert_fusion.1
  118.3 25.7 %reduce-scatter.5.cloned.1.call-done = bf16[128,1280]{1,0:T(8,128)(2,1)} async-done(((bf16[512,1280]{1,0:T(8,128)(2,1)}), bf16[128,1280]{1,0:T(8,128)(2,1)}) %reduce-scatter.5.cloned.1.call-update) | async-done | bytes 327696 | tf_op jit(solution)/shard_map/reduce_scatter | solution.py:71
  144.0 30.7 %reduce-scatter.3.cloned.1.call-done = bf16[128,1280]{1,0:T(8,128)(2,1)} async-done(((bf16[512,1280]{1,0:T(8,128)(2,1)}), bf16[128,1280]{1,0:T(8,128)(2,1)}) %reduce-scatter.3.cloned.1.call-update) | async-done | bytes 327696 | tf_op jit(solution)/shard_map/reduce_scatter | solution.py:70
  174.6 1.1 pad_maximum_fusion
  175.8 0.7 copy.35
  176.5 38.8 %all_to_all.31 = bf16[128,2,1280]{2,1,0:T(2,128)(2,1)S(1)} all-to-all(bf16[128,2,1280]{2,1,0:T(2,128)(2,1)S(1)} %copy.35), channel_id=1, replica_groups=mesh['expert'=128,'dp'=4] {'expert'}, dimensions={0} | all-to-all | bytes 1310720 | tf_op jit(solution)/shard_map/all_to_all | solution.py:74
  215.3 0.8 bitcast_reduce_fusion
  218.4 0.8 copy.38
  219.3 5.6 %all-to-all-start.2 = ((bf16[4,128,160]{1,2,0:T(8,128)(2,1)}), bf16[4,128,160]{1,2,0:T(8,128)(2,1)S(1)}, u32[]{:S(2)}, u32[]{:S(2)}) async-start(bf16[4,128,160]{1,2,0:T(8,128)(2,1)} %copy.38), calls=%async_computation.4 | async-start | bytes 327680 | tf_op jit(solution)/shard_map/all_to_all | solution.py:82
  224.9 3.3 %fusion.1 = bf16[1,1280,384]{2,1,0:T(8,128)(2,1)} fusion(bf16[512,384]{1,0:T(8,128)(2,1)S(1)} %get-tuple-element.12, bf16[512,1,1280]{2,0,1:T(8,128)(2,1)} %all-gather.7.cloned.1.call-done), kind=kOutput, calls=%fused_computation.5 | convolution fusion | flops 503808000 | bytes 2686976 | tf_op jit(solution)/shard_map/dot_general | solution.py:16
  228.1 1.8 fusion
  230.0 0.8 copy.39
  230.8 6.3 %all-to-all-start.3 = ((bf16[128,1,160]{2,1,0:T(2,128)(2,1)}), bf16[128,1,160]{2,1,0:T(2,128)(2,1)S(1)}, u32[]{:S(2)}, u32[]{:S(2)}) async-start(bf16[128,1,160]{2,1,0:T(2,128)(2,1)} %copy.39), calls=%async_computation.5 | async-start | bytes 262144 | tf_op jit(solution)/shard_map/all_to_all | solution.py:83
  237.1 12.8 %all-to-all-done.3 = bf16[128,1,160]{2,1,0:T(2,128)(2,1)S(1)} async-done(((bf16[128,1,160]{2,1,0:T(2,128)(2,1)}), bf16[128,1,160]{2,1,0:T(2,128)(2,1)S(1)}, u32[]{:S(2)}, u32[]{:S(2)}) %all-to-all-start.3) | async-done | bytes 40992 | tf_op jit(solution)/shard_map/all_to_all | solution.py:83
  250.1 0.7 broadcast_in_dim.12
  250.8 6.8 %all-to-all-start.4 = ((bf16[128,1,160]{2,1,0:T(2,128)(2,1)}), bf16[128,1,160]{2,1,0:T(2,128)(2,1)S(1)}, u32[]{:S(2)}, u32[]{:S(2)}) async-start(bf16[128,1,160]{2,1,0:T(2,128)(2,1)} %broadcast_in_dim.12), calls=%async_computation.6 | async-start | bytes 262144 | tf_op jit(solution)/shard_map/all_to_all | solution.py:85
  257.7 1.0 fusion.3
  258.7 11.9 %all-to-all-done.4 = bf16[128,1,160]{2,1,0:T(2,128)(2,1)S(1)} async-done(((bf16[128,1,160]{2,1,0:T(2,128)(2,1)}), bf16[128,1,160]{2,1,0:T(2,128)(2,1)S(1)}, u32[]{:S(2)}, u32[]{:S(2)}) %all-to-all-start.4) | async-done | bytes 40992 | tf_op jit(solution)/shard_map/all_to_all | solution.py:85
  270.9 0.7 reshape.74
  (48 shorter events, 4.1 us)
Async XLA Ops:
  7.2 73.6 %copy-start = (bf16[1,1280,384]{2,1,0:T(8,128)(2,1)S(1)}, bf16[1,1280,384]{2,1,0:T(8,128)(2,1)}, u32[]{:S(2)}) copy-start(bf16[1,1280,384]{2,1,0:T(8,128)(2,1)} %param.8) | copy-start | bytes 2949124
  7.2 5.0 %copy-start.3 = (bf16[1,128,1280]{2,1,0:T(8,128)(2,1)S(1)}, bf16[1,128,1280]{2,1,0:T(8,128)(2,1)}, u32[]{:S(2)}) copy-start(bf16[1,128,1280]{2,1,0:T(8,128)(2,1)} %param.6) | copy-start | bytes 983044
  7.2 73.6 %all-gather.5.cloned.1.call-start = ((), (), s32[]{:S(2)}) async-start(), calls=%async_computation.9 | async-start | bytes 1638400 | tf_op jit(solution)/shard_map/all_gather | solution.py:61
  58.1 53.3 %all-gather.7.cloned.1.call-start = ((), (), s32[]{:S(2)}) async-start(), calls=%async_computation.10 | async-start | bytes 1638400 | tf_op jit(solution)/shard_map/all_gather | solution.py:62
  58.9 52.5 %copy-start.4 = (bf16[1,1280,384]{2,1,0:T(8,128)(2,1)S(1)}, bf16[1,1280,384]{2,1,0:T(8,128)(2,1)}, u32[]{:S(2)}) copy-start(bf16[1,1280,384]{2,1,0:T(8,128)(2,1)} %param.9) | copy-start | bytes 2949124
  58.9 85.0 %reduce-scatter.5.cloned.1.call-start = ((), (), s32[]{:S(2)}) async-start(), calls=%async_computation.8 | async-start | bytes 1638400 | tf_op jit(solution)/shard_map/reduce_scatter | solution.py:71
  114.3 2.0 copy-start.5
  116.3 58.4 %reduce-scatter.3.cloned.1.call-start = ((), (), s32[]{:S(2)}) async-start(), calls=%async_computation.7 | async-start | bytes 1638400 | tf_op jit(solution)/shard_map/reduce_scatter | solution.py:70
  216.1 1.0 copy-start.1
  216.8 1.1 copy-start.2
  219.3 10.7 %all-to-all-start.2 = ((bf16[4,128,160]{1,2,0:T(8,128)(2,1)}), bf16[4,128,160]{1,2,0:T(8,128)(2,1)S(1)}, u32[]{:S(2)}, u32[]{:S(2)}) async-start(bf16[4,128,160]{1,2,0:T(8,128)(2,1)} %copy.38), calls=%async_computation.4 | async-start | bytes 327680 | tf_op jit(solution)/shard_map/all_to_all | solution.py:82
  224.8 3.3 %copy-start.6 = (bf16[512,384]{1,0:T(8,128)(2,1)S(1)}, bf16[512,384]{1,0:T(8,128)(2,1)}, u32[]{:S(2)}) copy-start(bf16[512,384]{1,0:T(8,128)(2,1)} %copy-done.5) | copy-start | bytes 1179652
  224.9 3.3 %copy-start.7 = (bf16[512,1,1280]{2,0,1:T(8,128)(2,1)S(1)}, bf16[512,1,1280]{2,0,1:T(8,128)(2,1)}, u32[]{:S(2)}) copy-start(bf16[512,1,1280]{2,0,1:T(8,128)(2,1)} %all-gather.5.cloned.1.call-done) | copy-start | bytes 3932164
  230.8 19.2 %all-to-all-start.3 = ((bf16[128,1,160]{2,1,0:T(2,128)(2,1)}), bf16[128,1,160]{2,1,0:T(2,128)(2,1)S(1)}, u32[]{:S(2)}, u32[]{:S(2)}) async-start(bf16[128,1,160]{2,1,0:T(2,128)(2,1)} %copy.39), calls=%async_computation.5 | async-start | bytes 262144 | tf_op jit(solution)/shard_map/all_to_all | solution.py:83
  250.8 19.7 %all-to-all-start.4 = ((bf16[128,1,160]{2,1,0:T(2,128)(2,1)}), bf16[128,1,160]{2,1,0:T(2,128)(2,1)S(1)}, u32[]{:S(2)}, u32[]{:S(2)}) async-start(bf16[128,1,160]{2,1,0:T(2,128)(2,1)} %broadcast_in_dim.12), calls=%async_computation.6 | async-start | bytes 262144 | tf_op jit(solution)/shard_map/all_to_all | solution.py:85
Sparse Core Ops, SparseCore 0:
  58.2 22.5 all-gather.4
  82.9 28.5 all-gather.6
  116.4 27.5 reduce-scatter.4
  146.7 27.9 reduce-scatter.2

commit v2 on v1

v2 whole, which is shorter than its diff:
```python
import functools

import jax
import jax.numpy as jnp
from jax import lax
from jax.experimental import pallas as pl
from jax.experimental.pallas import tpu as pltpu
from jax.sharding import PartitionSpec as P

logit_scale = 24.0
f32 = jnp.float32
bf16 = jnp.bfloat16
MESH = pl.DeviceIdType.MESH
N = 8
D = 1280
K = 384
HALF_D = 640


def dot(a, b, ca, cb):
    return lax.dot_general(a, b, (((ca,), (cb,)), ((), ())), preferred_element_type=f32)


def expert_of(k, j):
    return (j // 2) * 16 + (j % 2) * 2 + (k // 2) * 4 + k % 2


def k_of(e):
    return ((e // 4) % 4) * 2 + e % 2


def j_of(e):
    return (e // 16) * 2 + (e % 4) // 2


def pick(source):
    rows = lax.broadcasted_iota(jnp.int32, (128, 128), 0)
    cols = lax.broadcasted_iota(jnp.int32, (128, 128), 1)
    return jnp.where(source(rows) == cols, 1.0, 0.0).astype(bf16)


def by_member(o):
    k, h, j = o >> 4, (o >> 3) & 1, o & 7
    return h * 64 + (j >> 1) * 16 + (j & 1) * 2 + (k >> 1) * 4 + (k & 1)


def by_expert(o):
    h, e = o >> 6, o & 63
    k = ((e >> 2) & 3) * 2 + (e & 1)
    j = (e >> 4) * 2 + ((e >> 1) & 1)
    return k * 16 + h * 8 + j


def swapped(o):
    return (o & 7) * 16 + ((o >> 3) & 1) * 8 + (o >> 4)


def halves_out(o):
    return ((o >> 3) & 7) * 16 + (o >> 6) * 8 + (o & 7)


def halves_in(o):
    return ((o >> 3) & 1) * 64 + (o >> 4) * 8 + (o & 7)


def moved(source, value):
    return dot(pick(source), value, 1, 0).astype(bf16)


def to_row(column):
    return jnp.broadcast_to(column, (128, 128)).T[0:1, :]


def to_column(row):
    return jnp.broadcast_to(row, (128, 128)).T[:, 0:1]


def front(x, go, rt):
    xf = x.astype(f32)
    rf = rt.astype(f32)
    inv_x = to_row(lax.rsqrt(jnp.sum(xf * xf, axis=1, keepdims=True) + 1e-06))
    inv_r = lax.rsqrt(jnp.sum(rf * rf, axis=1, keepdims=True) + 1e-06)
    logits = (logit_scale * inv_x) * inv_r * dot(rt, x, 1, 1)
    e = jnp.exp(logits)
    disp = e / jnp.sum(e, axis=1, keepdims=True)
    comb = e / jnp.sum(e, axis=0, keepdims=True)
    slots = dot(disp.astype(bf16), x, 1, 0).astype(bf16)
    grads = dot(comb.astype(bf16), go, 1, 0).astype(bf16)
    return inv_x, inv_r, logits, disp, comb, slots, grads


def back(x, go, rt, saved, slots_out, grad_slots):
    inv_x, inv_r, logits, disp, comb = saved
    d_comb = dot(slots_out, go, 1, 1).astype(bf16).astype(f32)
    d_disp = dot(grad_slots, x, 1, 1).astype(bf16).astype(f32)
    d_log = disp * (d_disp - jnp.sum(disp * d_disp, axis=1, keepdims=True)) + comb * (
        d_comb - jnp.sum(comb * d_comb, axis=0, keepdims=True)
    )
    m = d_log * logits
    row = jnp.sum(m, axis=0, keepdims=True)
    col = jnp.sum(m, axis=1, keepdims=True)
    a = (logit_scale * inv_x) * inv_r * d_log
    hi = a.astype(bf16)
    lo = (a - hi.astype(f32)).astype(bf16)
    term = dot(jnp.concatenate([hi, lo], axis=0), x, 1, 0)
    term = term[:64] + term[64:] - rt.astype(f32) * (inv_r * inv_r * col)
    return hi, lo, row, term


def kernel(
    x_hbm, go_hbm, rt_hbm, wu_hbm, wd_hbm, gx_hbm, gr_hbm, gu_hbm, gd_hbm,
    x_ref, go_ref, rt_ref, wu_ref, wd_ref,
    s1, r1, s2, r2, xg, parts, sibr, cs, rz, ry, fy, fz, s3, r3, s4, r4,
    tp, q1, t2, q2, t3, q3, t4, ro, act_ref, dpre_ref, gx, gr, gu, gd,
    lsem, ssem, rsem,
):
    loads = [
        pltpu.make_async_copy(a, b, lsem.at[i])
        for i, (a, b) in enumerate(
            [(x_hbm, x_ref), (rt_hbm, rt_ref), (go_hbm, go_ref), (wu_hbm, wu_ref), (wd_hbm, wd_ref)]
        )
    ]
    for c in loads:
        c.start()

    ex, dp = lax.axis_index("expert"), lax.axis_index("dp")
    G, M = ex // 2, (ex % 2) * 4 + dp
    kG, jG = k_of(G), j_of(G)

    def dev(g, m):
        return {"expert": 2 * g + m // 4, "dp": m % 4}

    group = [(G, (M + d) % N) for d in range(1, N)]
    outs = [(expert_of(M, j), (G + j) % N) for j in range(N)]
    ins = [((M - jG + N) % N + N * i, kG) for i in range(N)]
    far = [(G % N + N * ((G // N + d) % N), M) for d in range(1, N)]
    near = [((G // N) * N + (G % N + d) % N, M) for d in range(1, N)]

    def is_me(g, m):
        return jnp.logical_and(g == G, m == M)

    barrier = pltpu.get_barrier_semaphore()
    for g, m in group + far + near:
        pl.semaphore_signal(barrier, inc=1, device_id=dev(g, m), device_id_type=MESH)
    for g, m in outs + ins:

        @pl.when(jnp.logical_not(is_me(g, m)))
        def _():
            pl.semaphore_signal(barrier, inc=1, device_id=dev(g, m), device_id_type=MESH)

    mine = jnp.logical_and(kG == M, (G + jG) % N == M).astype(jnp.int32)

    sems = [0]
    pending = []

    def sems_of(n):
        at = sems[0]
        sems[0] += n
        return at

    def copy(src, dst, s, r, to):
        return pltpu.make_async_remote_copy(
            src_ref=src, dst_ref=dst, send_sem=ssem.at[s], recv_sem=rsem.at[r],
            device_id=dev(*to), device_id_type=MESH,
        )

    def all_to_all(src, dst):
        at = sems_of(N - 1)
        for d in range(1, N):
            to = (G, (M + d) % N)
            c = copy(src.at[to[1]], dst.at[M], at + d - 1, at + d - 1, to)
            c.start()
            pending.append((c, None))
        dst[M] = src[M]
        for d in range(1, N):
            came = (M - d + N) % N
            copy(src.at[came], dst.at[came], at + d - 1, at + d - 1, (G, came)).wait_recv()

    def exchange(src, dst, partners, slot, n):
        at = sems_of(n - 1)
        for d in range(1, n):
            c = copy(src, dst.at[slot], at + d - 1, at + d - 1, partners[d - 1])
            c.start()
            pending.append((c, None))
        dst[slot] = src[...]
        for d in range(1, n):
            came = (slot - d + n) % n
            copy(src, dst.at[came], at + d - 1, at + d - 1, partners[d - 1]).wait_recv()

    def cross(src, dst, to, slot, sources):
        at = sems_of(N)
        for b in range(N):
            c = copy(src.at[b], dst.at[slot], at + b, at + slot, to[b])
            me = is_me(*to[b])

            @pl.when(me)
            def _():
                dst[slot] = src[b]

            @pl.when(jnp.logical_not(me))
            def _():
                c.start()

            pending.append((c, me))
        for b in range(N):

            @pl.when(jnp.logical_not(is_me(*sources[b])))
            def _():
                copy(src.at[b], dst.at[b], at + b, at + b, sources[b]).wait_recv()

    def send(src, dst, to):
        at = sems_of(1)
        c = copy(src, dst, at, at, to)
        c.start()
        pending.append((c, None))
        return c

    for c in loads[:3]:
        c.wait()
    x, go, rt = x_ref[...], go_ref[...], rt_ref[...]
    *saved, slots, grads = front(x, go, rt)
    s1[...] = moved(by_member, jnp.concatenate([slots, grads], axis=0)).reshape(N, 16, D)
    pl.semaphore_wait(barrier, 7 * 3 + 16 - 2 * mine)

    all_to_all(s1, r1)
    s2[...] = moved(swapped, r1[...].reshape(128, D)).reshape(N, 16, D)
    cross(s2, r2, outs, G // N, ins)
    xg[M] = moved(halves_out, r2[...].reshape(128, D))

    my, mz = (M + 4) % N, M + 2 - 4 * ((M // 2) % 2)
    md = (mz + 4) % N

    def sib(m):
        return m + 1 - 2 * (m % 2)

    Y, Z, S = (G, my), (G, mz), (G, sib(M))
    top, low = pl.ds(0, 64), pl.ds(64, 64)
    own_y = send(xg.at[M], xg.at[M], Y)
    own_z = send(xg.at[M], xg.at[M], Z)
    own_s = send(xg.at[M], xg.at[M], S)
    own_y.wait_recv()
    ty = send(xg.at[my, top], xg.at[my, top], Z)
    sy = send(xg.at[my], xg.at[my], S)
    own_z.wait_recv()
    tz = send(xg.at[mz, low], xg.at[mz, low], Y)
    sz = send(xg.at[mz], xg.at[mz], S)
    ty.wait_recv()
    sd = send(xg.at[md, top], xg.at[md, top], S)
    tz.wait_recv()
    se = send(xg.at[md, low], xg.at[md, low], S)
    for c in (own_s, sy, sz, sd, se):
        c.wait_recv()

    loads[3].wait()
    loads[4].wait()

    @pl.loop(0, 4)
    def _(b):
        wu, wd = wu_ref[...], wd_ref[...]
        rows = xg[pl.ds(2 * b, 2), 0:64, :].reshape(128, D)
        grows = xg[pl.ds(2 * b, 2), 64:128, :].reshape(128, D)
        pre = dot(rows, wu, 1, 0)
        cdf = 0.5 * (1.0 + lax.erf(pre * 0.7071067811865476))
        pdf = 0.3989422804014327 * jnp.exp(-0.5 * pre * pre)
        act = (pre * cdf).astype(bf16)
        dpre = (dot(grows, wd, 1, 0) * (cdf + pre * pdf)).astype(bf16)
        at = pl.ds(pl.multiple_of(b * 128, 128), 128)
        act_ref[at, :] = act
        dpre_ref[at, :] = dpre
        parts[pl.ds(2 * b, 2), 0:64, :] = dot(act, wd, 1, 1).astype(bf16).reshape(2, 64, D)
        parts[pl.ds(2 * b, 2), 64:128, :] = dot(dpre, wu, 1, 1).astype(bf16).reshape(2, 64, D)

    order = (M, my, mz, md)
    to_sib = {q: send(parts.at[sib(order[q])], sibr.at[q], S) for q in (3, 1, 2, 0)}

    def chip_sum(q):
        to_sib[q].wait_recv()
        return parts[order[q]].astype(f32) + sibr[q].astype(f32)

    cs[3] = chip_sum(3).astype(bf16)
    dz = send(cs.at[3, top], rz, Z)
    dy = send(cs.at[3, low], ry, Y)
    v = chip_sum(1)
    dz.wait_recv()
    cs[1, 0:64, :] = (v[0:64] + rz[...].astype(f32)).astype(bf16)
    cs[1, 64:128, :] = v[64:128].astype(bf16)
    to_y = send(cs.at[1], fy, Y)
    v = chip_sum(2)
    dy.wait_recv()
    cs[2, 0:64, :] = v[0:64].astype(bf16)
    cs[2, 64:128, :] = (v[64:128] + ry[...].astype(f32)).astype(bf16)
    to_z = send(cs.at[2], fz, Z)

    grows = xg[:, 64:128, :].reshape(512, D)
    gd[...] = dot(grows, act_ref[...], 0, 0).astype(bf16)
    rows = xg[:, 0:64, :].reshape(512, D)
    gu[...] = dot(rows, dpre_ref[...], 0, 0).astype(bf16)
    stores = [
        pltpu.make_async_copy(gu, gu_hbm, lsem.at[5]),
        pltpu.make_async_copy(gd, gd_hbm, lsem.at[6]),
    ]
    for c in stores:
        c.start()

    v = chip_sum(0)
    to_y.wait_recv()
    to_z.wait_recv()
    total = (v + fy[...].astype(f32) + fz[...].astype(f32)).astype(bf16)

    s3[...] = moved(halves_in, total).reshape(N, 16, D)
    cross(s3, r3, ins, jG, outs)
    s4[...] = moved(swapped, r3[...].reshape(128, D)).reshape(N, 16, D)
    all_to_all(s4, r4)
    got = moved(by_expert, r4[...].reshape(128, D))
    slots_out, grad_slots = got[:64], got[64:]
    x, go, rt = x_ref[...], go_ref[...], rt_ref[...]
    hi, lo, row, term = back(x, go, rt, saved, slots_out, grad_slots)

    tb = term.astype(bf16)
    for m in range(N):
        r, zl = (m // 4) * 2 + m % 2, (m // 2) % 2
        tp[m] = tb[16 * r : 16 * r + 16, HALF_D * zl : HALF_D * (zl + 1)]
    all_to_all(tp, q1)

    left = jnp.concatenate([saved[3].astype(bf16), hi, lo], axis=0)
    right = jnp.concatenate([grad_slots, rt, rt], axis=0)
    inv_x = saved[0]
    gx[...] = (dot(left, right, 0, 0) - x.astype(f32) * to_column(inv_x * inv_x * row)).astype(bf16)
    out_x = pltpu.make_async_copy(gx, gx_hbm, lsem.at[7])
    out_x.start()
    stores.append(out_x)

    t2[...] = jnp.sum(q1[...].astype(f32), axis=0).astype(bf16)
    exchange(t2, q2, far, G // N, N)
    t3[...] = jnp.sum(q2[...].astype(f32), axis=0).astype(bf16)
    exchange(t3, q3, near, G % N, N)
    t4[...] = jnp.sum(q3[...].astype(f32), axis=0).astype(bf16)
    r, zl = (M // 4) * 2 + M % 2, (M // 2) % 2
    same = [(r + d) % 4 for d in range(1, 4)]
    exchange(t4, ro, [(G, (a // 2) * 4 + zl * 2 + a % 2) for a in same], r, 4)
    whole = ro[...].reshape(64, HALF_D).astype(f32)
    gr[...] = jnp.where(M % 2 == 0, whole[:, :320], whole[:, 320:])
    out_r = pltpu.make_async_copy(gr, gr_hbm, lsem.at[8])
    out_r.start()
    stores.append(out_r)

    for c, me in pending:
        if me is None:
            c.wait_send()
        else:
            pl.when(jnp.logical_not(me))(c.wait_send)
    for c in stores:
        c.wait()


N_SEMS = 7 + 8 + 9 + 8 + 8 + 7 + 7 + 7 + 7 + 3


def local(tokens, grad_out, router, up_weight, down_weight):
    block = pltpu.VMEM((N, 16, D), bf16)
    big = pltpu.VMEM((N, 128, D), bf16)
    piece = pltpu.VMEM((N, 16, HALF_D), bf16)
    one = pltpu.VMEM((16, HALF_D), bf16)
    weight = pltpu.VMEM((D, K), bf16)
    image = pltpu.VMEM((128, D), bf16)
    scratch = [
        image, image, pltpu.VMEM((64, D), bf16), weight, weight,
        block, block, block, block, big, big,
        pltpu.VMEM((4, 128, D), bf16), pltpu.VMEM((4, 128, D), bf16),
        pltpu.VMEM((64, D), bf16), pltpu.VMEM((64, D), bf16), image, image,
        block, block, block, block,
        piece, piece, one, piece, one, piece, one, pltpu.VMEM((4, 16, HALF_D), bf16),
        pltpu.VMEM((512, K), bf16), pltpu.VMEM((512, K), bf16),
        image, pltpu.VMEM((64, 320), f32), weight, weight,
        pltpu.SemaphoreType.DMA((9,)),
        pltpu.SemaphoreType.DMA((N_SEMS,)),
        pltpu.SemaphoreType.DMA((N_SEMS,)),
    ]
    anywhere = pl.BlockSpec(memory_space=pl.ANY)
    gx, gr, gu, gd = pl.pallas_call(
        kernel,
        out_shape=(
            jax.ShapeDtypeStruct((128, D), bf16),
            jax.ShapeDtypeStruct((64, 320), f32),
            jax.ShapeDtypeStruct((D, K), bf16),
            jax.ShapeDtypeStruct((D, K), bf16),
        ),
        in_specs=[anywhere] * 5,
        out_specs=(anywhere,) * 4,
        scratch_shapes=scratch,
        compiler_params=pltpu.CompilerParams(
            collective_id=0, has_side_effects=True, vmem_limit_bytes=56 * 2**20
        ),
        cost_estimate=pl.CostEstimate(flops=4 * 10**9, bytes_accessed=6 * 10**6, transcendentals=500000),
    )(tokens[0], grad_out[0], router.T, up_weight[0], down_weight[0])
    return (gx[None], gr.T, gu[None], gd[None])


def solution(mesh):
    placed = (
        P(("expert", "dp"), None, None),
        P(("expert", "dp"), None, None),
        P(),
        P("expert", None, "dp"),
        P("expert", None, "dp"),
    )
    return jax.shard_map(
        local,
        mesh=mesh,
        in_specs=placed,
        out_specs=(
            P(("expert", "dp"), None, None),
            P("dp", None),
            P("expert", None, "dp"),
            P("expert", None, "dp"),
        ),
        check_vma=False,
    )
```

time: 279 us -> 139 us (0.50)
  Pallas kernels: 0 us -> 132 us
  waiting for transfers between devices: 129 us -> 0 us
  blocking collectives: 82.1 us -> 0 us
  matrix products: 21.1 us -> 0 us
  starting transfers between devices: 18.9 us -> 0 us
  between operations: 14 us -> 0.65 us
  other arithmetic: 5.28 us -> 0 us
    pallas_call x0 -> x1, Pallas kernels: none -> 132 us  [local(): pl.pallas_call(kernel, out_shape=(jax.ShapeDtypeStruct((128, D), bf16), j...]
    all_to_all x2 -> x0, blocking collectives: 82.1 us -> none  [the longest x1 43.2 us: local(): lax.all_to_all(sent, 'expert', split_axis=0, concat_axis=0, tiled=True)]
    reduce_scatter x2 -> x0, waiting for transfers between devices: 56.3 us -> none  [the longest x1 30.7 us: local(): y = lax.psum_scatter(part_y, 'dp', scatter_dimension=0, tiled=True)]
    all_gather x2 -> x0, waiting for transfers between devices: 47.7 us -> none  [the longest x1 25.9 us: local(): grows = lax.all_gather(got[:, 1], 'dp', axis=0, tiled=True)]
    all_to_all x3 -> x0, waiting for transfers between devices: 24.7 us -> none  [the longest x1 12.8 us: local(): own = lax.all_to_all(own.astype(bf16), 'expert', 0, 0, tiled=True)]
    dot_general x13 -> x0, matrix products: 21.1 us -> none  [dot(): lax.dot_general(a, b, (((ca,), (cb,)), ((), ())), preferred_element_type=...]
    all_to_all x3 -> x0, starting transfers between devices: 18.8 us -> none  [the longest x1 6.83 us: local(): lax.all_to_all(jnp.broadcast_to(own, (n_ex, own.shape[0])), 'expert', 0,...]
    unnamed x19 -> x8, local copies, waits for them, and re-layouts: 1.83 us -> 5.67 us
  transfers between devices with their start and end apart: 7 -> 0, of which waited for: 6 -> 0; matrix products, arithmetic and copies ran while one was open for 5% -> 0% of each run, Pallas kernels for 0% -> 0%
where the time goes in v2:
time: 139 us
  Pallas kernels  132 us (95%)
  local copies, waits for them, and re-layouts  5.67 us (4%)
    pallas_call x1, Pallas kernels, local(): pl.pallas_call(kernel, out_shape=(jax.ShapeDtypeStruct((128, D), bf16), j...  132 us
    unnamed x8, local copies, waits for them, and re-layouts  5.67 us

profile of v2, /device:TPU:1, one launch (start us, length us, event | category | flops | bytes accessed | tf_op | source)
XLA Modules:
  0.0 138.7 jit_solution(11907263643500087786)
XLA Ops:
  0.6 132.4 %shard_map.84 = (bf16[128,1280]{1,0:T(8,128)(2,1)}, f32[64,320]{1,0:T(8,128)}, bf16[1280,384]{1,0:T(8,128)(2,1)}, bf16[1280,384]{1,0:T(8,128)(2,1)}) custom-call(bf16[128,1280]{1,0:T(8,128)(2,1)} %bitcast.15, bf16[128,1280]{1,0:T(8,128)(2,1)} %bitcast.16, bf16[64,1280]{1,0:T(8,128)(2,1)} %bitcast.17, bf16[1280,384]{1,0:T(8,128)(2,1)} %bitcast.13, ...), custom_call_target="tpu_custom_call" | custom-call | flops 4000000000 | bytes 6000000 | tf_op jit(solution)/shard_map/pallas_call | solution.py:380
  133.0 0.0 copy-start.1
  133.0 1.8 %copy.13 = bf16[1,128,1280]{2,1,0:T(8,128)(2,1)} copy(bf16[1,128,1280]{2,1,0:T(8,128)(2,1)} %bitcast.11) | data formatting | bytes 655360
  134.8 0.0 copy-done.1
  134.8 0.6 copy.14
  135.4 0.0 copy-start
  135.4 2.3 %copy.15 = bf16[1,1280,384]{2,1,0:T(8,128)(2,1)} copy(bf16[1,1280,384]{2,1,0:T(8,128)(2,1)} %bitcast.10) | data formatting | bytes 1966080
  137.8 0.0 copy-done
  137.8 0.9 copy.16
Async XLA Ops:
  133.0 1.8 %copy-start.1 = (f32[64,320]{1,0:T(8,128)S(1)}, f32[64,320]{1,0:T(8,128)}, u32[]{:S(2)}) copy-start(f32[64,320]{1,0:T(8,128)} %get-tuple-element.9) | copy-start | bytes 245764
  135.4 2.3 %copy-start = (bf16[1280,384]{1,0:T(8,128)(2,1)S(1)}, bf16[1280,384]{1,0:T(8,128)(2,1)}, u32[]{:S(2)}) copy-start(bf16[1280,384]{1,0:T(8,128)(2,1)} %get-tuple-element.11) | copy-start | bytes 2949124

commit v3 on v2

v3 whole, which is shorter than its diff:
```python
import functools

import jax
import jax.numpy as jnp
from jax import lax
from jax.experimental import pallas as pl
from jax.experimental.pallas import tpu as pltpu
from jax.sharding import PartitionSpec as P

logit_scale = 24.0
f32 = jnp.float32
bf16 = jnp.bfloat16
MESH = pl.DeviceIdType.MESH
N = 8
D = 1280
K = 384
HALF_D = 640


def dot(a, b, ca, cb):
    return lax.dot_general(a, b, (((ca,), (cb,)), ((), ())), preferred_element_type=f32)


def bits(m):
    return m // 4, (m // 2) % 2, m % 2


def flip(bit, by):
    return 1 - bit if by else bit


def step(g, dz, dx, dy):
    z, x, y = g // 16, (g // 4) % 4, g % 4
    return ((z + dz) % 4) * 16 + ((x + dx) % 4) * 4 + (y + dy) % 4


def receiver(g, m, j):
    yl, zl, c = bits(m)
    b, odd, dx1 = j // 4, 1 - (j // 2) % 2, j % 2
    dx0 = c * b + (1 - c) * flip(yl, b)
    dy = c * (3 - 2 * yl) + (1 - c) * 2 * b
    dz = 3 - 2 * zl if odd else 2 * flip(zl, dx1)
    to_y = c * (1 - yl) + (1 - c) * flip(yl, b)
    to_z = 1 - zl if odd else dx1
    i = b * 4 + (1 - odd) * 2 + flip(zl, dx1)
    return step(g, dz, dx1 * 2 + dx0, dy), to_y * 4 + to_z * 2 + c, i


def sender(e, t, i):
    yl, zl, c = bits(t)
    b, odd, q = i // 4, 1 - (i // 2) % 2, i % 2
    dx1 = flip(1 - zl, q) if odd else zl
    dz = 1 + 2 * zl if odd else 2 * q
    dy = c * (1 + 2 * yl) + (1 - c) * 2 * b
    dx0 = c * b + (1 - c) * yl
    from_y = c * (1 - yl) + (1 - c) * flip(yl, b)
    from_z = 1 - zl if odd else flip(zl, q)
    j = b * 4 + (1 - odd) * 2 + dx1
    return step(e, 4 - dz, 4 - (dx1 * 2 + dx0), 4 - dy), from_y * 4 + from_z * 2 + c, j


SELF = 2


def by_expert(g):
    def source(o):
        h, e = o >> 6, o & 63
        dz = ((e >> 4) - g // 16) & 3
        dx = ((e >> 2) - g // 4) & 3
        dy = (e - g) & 3
        dx0, dx1, c, odd = dx & 1, dx >> 1, dy & 1, dz & 1
        yl = c * (1 - (dy >> 1)) + (1 - c) * ((dy >> 1) ^ dx0)
        zl = odd * (1 - (dz >> 1)) + (1 - odd) * ((dz >> 1) ^ dx1)
        b = c * dx0 + (1 - c) * (dy >> 1)
        j = b * 4 + (1 - odd) * 2 + dx1
        return (yl * 4 + zl * 2 + c) * 16 + h * 8 + j

    return source


def pick(source, inverse=False):
    rows = lax.broadcasted_iota(jnp.int32, (128, 128), 0)
    cols = lax.broadcasted_iota(jnp.int32, (128, 128), 1)
    hit = rows == source(cols) if inverse else source(rows) == cols
    return jnp.where(hit, 1.0, 0.0).astype(bf16)


def swapped(o):
    return (o & 7) * 16 + ((o >> 3) & 1) * 8 + (o >> 4)


def moved(source, value, inverse=False):
    return dot(pick(source, inverse), value, 1, 0).astype(bf16)


def to_row(column):
    return jnp.broadcast_to(column, (128, 128)).T[0:1, :]


def to_column(row):
    return jnp.broadcast_to(row, (128, 128)).T[:, 0:1]


def front(x, go, rt):
    xf = x.astype(f32)
    rf = rt.astype(f32)
    inv_x = to_row(lax.rsqrt(jnp.sum(xf * xf, axis=1, keepdims=True) + 1e-06))
    inv_r = lax.rsqrt(jnp.sum(rf * rf, axis=1, keepdims=True) + 1e-06)
    logits = (logit_scale * inv_x) * inv_r * dot(rt, x, 1, 1)
    e = jnp.exp(logits)
    disp = e / jnp.sum(e, axis=1, keepdims=True)
    comb = e / jnp.sum(e, axis=0, keepdims=True)
    slots = dot(disp.astype(bf16), x, 1, 0).astype(bf16)
    grads = dot(comb.astype(bf16), go, 1, 0).astype(bf16)
    return inv_x, inv_r, logits, disp, comb, slots, grads


def back(x, go, rt, saved, slots_out, grad_slots):
    inv_x, inv_r, logits, disp, comb = saved
    d_comb = dot(slots_out, go, 1, 1).astype(bf16).astype(f32)
    d_disp = dot(grad_slots, x, 1, 1).astype(bf16).astype(f32)
    d_log = disp * (d_disp - jnp.sum(disp * d_disp, axis=1, keepdims=True)) + comb * (
        d_comb - jnp.sum(comb * d_comb, axis=0, keepdims=True)
    )
    m = d_log * logits
    row = jnp.sum(m, axis=0, keepdims=True)
    col = jnp.sum(m, axis=1, keepdims=True)
    a = (logit_scale * inv_x) * inv_r * d_log
    hi = a.astype(bf16)
    lo = (a - hi.astype(f32)).astype(bf16)
    term = dot(jnp.concatenate([hi, lo], axis=0), x, 1, 0)
    term = term[:64] + term[64:] - rt.astype(f32) * (inv_r * inv_r * col)
    return hi, lo, row, term


def kernel(
    x_hbm, go_hbm, rt_hbm, wu_hbm, wd_hbm, gx_hbm, gr_hbm, gu_hbm, gd_hbm,
    x_ref, go_ref, rt_ref, wu_ref, wd_ref,
    s1, r1, s2, xg, xs, gs, parts, sibr, cs, rel, fy, fz, s3, r3, s4, r4,
    tp, q1, t2, q2, t3, q3, t4, ro, act_ref, dpre_ref, gx, gr, gu, gd,
    lsem, ssem, rsem,
):
    loads = [
        pltpu.make_async_copy(a, b, lsem.at[i])
        for i, (a, b) in enumerate(
            [(x_hbm, x_ref), (rt_hbm, rt_ref), (go_hbm, go_ref), (wu_hbm, wu_ref), (wd_hbm, wd_ref)]
        )
    ]
    for c in loads:
        c.start()

    ex, dp = lax.axis_index("expert"), lax.axis_index("dp")
    G, M = ex // 2, (ex % 2) * 4 + dp

    def dev(g, m):
        return {"expert": 2 * g + m // 4, "dp": m % 4}

    group = [(G, (M + d) % N) for d in range(1, N)]
    outs = [receiver(G, M, j) for j in range(N)]
    ins = [sender(G, M, i) for i in range(N)]
    far = [(G % N + N * ((G // N + d) % N), M) for d in range(1, N)]
    near = [((G // N) * N + (G % N + d) % N, M) for d in range(1, N)]
    keeps = M == 0

    barrier = pltpu.get_barrier_semaphore()

    def greet(g, m):
        pl.semaphore_signal(barrier, inc=1, device_id=dev(g, m), device_id_type=MESH)

    for g, m in group + far + near:
        greet(g, m)
    for n in range(N):
        for g, m, _ in (outs[n], ins[n]):
            if n == SELF:
                pl.when(jnp.logical_not(keeps))(functools.partial(greet, g, m))
            else:
                greet(g, m)

    sems = [0]
    pending = []

    def sems_of(n):
        at = sems[0]
        sems[0] += n
        return at

    def copy(src, dst, s, r, to):
        return pltpu.make_async_remote_copy(
            src_ref=src, dst_ref=dst, send_sem=ssem.at[s], recv_sem=rsem.at[r],
            device_id=dev(*to), device_id_type=MESH,
        )

    def all_to_all(src, dst):
        at = sems_of(N - 1)
        for d in range(1, N):
            to = (G, (M + d) % N)
            c = copy(src.at[to[1]], dst.at[M], at + d - 1, at + d - 1, to)
            c.start()
            pending.append((c, None))
        dst[M] = src[M]

        def wait():
            for d in range(1, N):
                came = (M - d + N) % N
                copy(src.at[came], dst.at[came], at + d - 1, at + d - 1, (G, came)).wait_recv()

        return wait

    def exchange(src, dst, partners, slot, n):
        at = sems_of(n - 1)
        for d in range(1, n):
            c = copy(src, dst.at[slot], at + d - 1, at + d - 1, partners[d - 1])
            c.start()
            pending.append((c, None))
        dst[slot] = src[...]
        for d in range(1, n):
            came = (slot - d + n) % n
            copy(src, dst.at[came], at + d - 1, at + d - 1, partners[d - 1]).wait_recv()

    def unless(me, do):
        if me is None:
            do()
        else:
            pl.when(jnp.logical_not(me))(do)

    def cross_send(at, n, src, dst, own, to):
        c = copy(src, dst, at + n, at + to[2], to[:2])
        me = keeps if n == SELF else None
        unless(me, c.start)
        if me is not None:

            @pl.when(me)
            def _():
                own[...] = src[...]

        pending.append((c, me))

    def cross_wait(at, n, dst, source):
        unless(keeps if n == SELF else None, copy(dst, dst, at + n, at + n, source[:2]).wait_recv)

    def send(src, dst, to):
        at = sems_of(1)
        c = copy(src, dst, at, at, to)
        c.start()
        pending.append((c, None))
        return c

    for c in loads[:3]:
        c.wait()
    x, go, rt = x_ref[...], go_ref[...], rt_ref[...]
    *saved, slots, grads = front(x, go, rt)
    slotted = jnp.concatenate([slots, grads], axis=0)
    s1[...] = moved(by_expert(G), slotted, inverse=True).reshape(N, 16, D)
    pl.semaphore_wait(barrier, 7 * 3 + 16 - 2 * (1 - jnp.minimum(M, 1)))

    all_to_all(s1, r1)()
    s2[...] = moved(swapped, r1[...].reshape(128, D)).reshape(N, 16, D)
    at2, at3 = sems_of(N), sems_of(N)
    for j in range(N):
        g, t, i = outs[j]
        cross_send(at2, j, s2.at[j], xg.at[t, i], xg.at[M, SELF], outs[j])

    yl, zl, c0 = bits(M)
    my, mz, md = M + 4 - 8 * yl, M + 2 - 4 * zl, 7 - M + 2 * c0 - 1
    ms = 1 - 2 * c0
    chip, chip_y, chip_z, chip_d = M // 2, my // 2, mz // 2, md // 2
    Y, Z, S = (G, my), (G, mz), (G, M + ms)
    marks = {}

    def rows_of(m, q):
        return xg.at[m, pl.ds(2 * q, 2)]

    def spread(m, q, name, to):
        marks[name, q] = send(rows_of(m, q), rows_of(m, q), to)

    def stage_a(q):
        for i in (2 * q, 2 * q + 1):
            cross_wait(at2, i, xg.at[M, i], ins[i])
        spread(M, q, "y", Y)
        spread(M, q, "z", Z)
        spread(M, q, "s", S)

    def stage_b(q):
        marks["y", q].wait_recv()
        if q < 2:
            spread(my, q, "d", Z)
        spread(my, q, "sy", S)
        marks["z", q].wait_recv()
        if q >= 2:
            spread(mz, q, "d", Y)
        spread(mz, q, "sz", S)

    def stage_c(q):
        marks["d", q].wait_recv()
        spread(md, q, "sd", S)

    def stage_d(q):
        for name in ("s", "sy", "sz", "sd"):
            marks[name, q].wait_recv()
        if q == 0:
            loads[3].wait()
            loads[4].wait()
        wu, wd = wu_ref[...], wd_ref[...]
        both = xg[:, 2 * q : 2 * q + 2].astype(f32).reshape(16, 2, 8, D)
        rows = both[:, 0].reshape(128, D).astype(bf16)
        grows = both[:, 1].reshape(128, D).astype(bf16)
        at = slice(128 * q, 128 * q + 128)
        xs[at, :] = rows
        gs[at, :] = grows
        pre = dot(rows, wu, 1, 0)
        cdf = 0.5 * (1.0 + lax.erf(pre * 0.7071067811865476))
        pdf = 0.3989422804014327 * jnp.exp(-0.5 * pre * pre)
        act = (pre * cdf).astype(bf16)
        dpre = (dot(grows, wd, 1, 0) * (cdf + pre * pdf)).astype(bf16)
        act_ref[at, :] = act
        dpre_ref[at, :] = dpre
        out = dot(act, wd, 1, 1).reshape(16, 1, 8, D)
        back_out = dot(dpre, wu, 1, 1).reshape(16, 1, 8, D)
        mixed = jnp.concatenate([out, back_out], axis=1).reshape(16, 16, D).astype(bf16)
        parts[q] = mixed.reshape(4, 2, 2, 16, D)
        marks["p", q] = send(parts.at[q, :, 1 - c0], sibr.at[q], S)

    def chip_sum(q, to):
        return parts[q, to, c0].astype(f32) + sibr[q, to].astype(f32)

    def forward(q, n, value, dst, name, to):
        cs[q, n] = value.astype(bf16)
        marks[name, q] = send(cs.at[q, n], dst.at[q], to)

    def stage_e(q):
        marks["p", q].wait_recv()
        diagonal = chip_sum(q, chip_d)
        if q < 2:
            forward(q, 0, diagonal, rel, "r", Z)
            forward(q, 1, chip_sum(q, chip_z), fz, "fz", Z)
        else:
            forward(q, 0, diagonal, rel, "r", Y)
            forward(q, 1, chip_sum(q, chip_y), fy, "fy", Y)

    def stage_f(q):
        marks["r", q].wait_recv()
        if q < 2:
            forward(q, 2, chip_sum(q, chip_y) + rel[q].astype(f32), fy, "fy", Y)
        else:
            forward(q, 2, chip_sum(q, chip_z) + rel[q].astype(f32), fz, "fz", Z)

    def stage_g(q):
        marks["fy", q].wait_recv()
        marks["fz", q].wait_recv()
        total = chip_sum(q, chip) + fy[q].astype(f32) + fz[q].astype(f32)
        s3[2 * q : 2 * q + 2] = total.astype(bf16)
        for i in (2 * q, 2 * q + 1):
            g, t, j = ins[i]
            cross_send(at3, i, s3.at[i], r3.at[j], r3.at[SELF], ins[i])

    chain = ((stage_a, 0), (stage_b, 1), (stage_c, 2), (stage_e, 4), (stage_f, 5), (stage_g, 6), (stage_d, 3))
    for t in range(4 + 6):
        for run, late in chain:
            if 0 <= t - late < 4:
                run(t - late)

    gd[...] = dot(gs[...], act_ref[...], 0, 0).astype(bf16)
    stores = [pltpu.make_async_copy(gd, gd_hbm, lsem.at[6])]
    stores[0].start()

    for j in range(N):
        cross_wait(at3, j, r3.at[j], outs[j])
    s4[...] = moved(swapped, r3[...].reshape(128, D)).reshape(N, 16, D)
    wait = all_to_all(s4, r4)
    gu[...] = dot(xs[...], dpre_ref[...], 0, 0).astype(bf16)
    stores.append(pltpu.make_async_copy(gu, gu_hbm, lsem.at[5]))
    stores[1].start()
    wait()
    got = moved(by_expert(G), r4[...].reshape(128, D))
    slots_out, grad_slots = got[:64], got[64:]
    x, go, rt = x_ref[...], go_ref[...], rt_ref[...]
    hi, lo, row, term = back(x, go, rt, saved, slots_out, grad_slots)

    tb = term.astype(bf16)
    for m in range(N):
        r, zh = (m // 4) * 2 + m % 2, (m // 2) % 2
        tp[m] = tb[16 * r : 16 * r + 16, HALF_D * zh : HALF_D * (zh + 1)]
    wait = all_to_all(tp, q1)

    left = jnp.concatenate([saved[3].astype(bf16), hi, lo], axis=0)
    right = jnp.concatenate([grad_slots, rt, rt], axis=0)
    inv_x = saved[0]
    gx[...] = (dot(left, right, 0, 0) - x.astype(f32) * to_column(inv_x * inv_x * row)).astype(bf16)
    stores.append(pltpu.make_async_copy(gx, gx_hbm, lsem.at[7]))
    stores[2].start()
    wait()
    t2[...] = jnp.sum(q1[...].astype(f32), axis=0).astype(bf16)
    exchange(t2, q2, far, G // N, N)
    t3[...] = jnp.sum(q2[...].astype(f32), axis=0).astype(bf16)
    exchange(t3, q3, near, G % N, N)
    t4[...] = jnp.sum(q3[...].astype(f32), axis=0).astype(bf16)
    r = yl * 2 + c0
    same = [(r + d) % 4 for d in range(1, 4)]
    exchange(t4, ro, [(G, (a // 2) * 4 + zl * 2 + a % 2) for a in same], r, 4)
    whole = ro[...].reshape(64, HALF_D).astype(f32)
    gr[...] = jnp.where(c0 == 0, whole[:, :320], whole[:, 320:])
    stores.append(pltpu.make_async_copy(gr, gr_hbm, lsem.at[8]))
    stores[3].start()

    for c, me in pending:
        unless(me, c.wait_send)
    for c in stores:
        c.wait()


def keep(*refs):
    ins, outs, bufs, sem = refs[:4], refs[4:8], refs[8:12], refs[12]
    parts = [(n, h) for n in (2, 3, 0, 1) for h in (0, 1)]

    def part(ref, h):
        half = ref.shape[0] // 2
        return ref.at[pl.ds(h * half, half)]

    reads = [
        pltpu.make_async_copy(part(ins[n], h), part(bufs[n], h), sem.at[0, n, h]) for n, h in parts
    ]
    writes = [
        pltpu.make_async_copy(part(bufs[n], h), part(outs[n], h), sem.at[1, n, h]) for n, h in parts
    ]
    for one in reads:
        one.start()
    for one, two in zip(reads, writes):
        one.wait()
        two.start()
    for two in writes:
        two.wait()


N_SEMS = 7 + 8 + 8 + 4 * (7 + 4) + 7 + 7 + 7 + 7 + 3


def local(tokens, grad_out, router, up_weight, down_weight):
    block = pltpu.VMEM((N, 16, D), bf16)
    piece = pltpu.VMEM((N, 16, HALF_D), bf16)
    one = pltpu.VMEM((16, HALF_D), bf16)
    weight = pltpu.VMEM((D, K), bf16)
    image = pltpu.VMEM((128, D), bf16)
    four = pltpu.VMEM((4, 2, 16, D), bf16)
    scratch = [
        image, image, pltpu.VMEM((64, D), bf16), weight, weight,
        block, block, block, pltpu.VMEM((N, N, 16, D), bf16),
        pltpu.VMEM((512, D), bf16), pltpu.VMEM((512, D), bf16),
        pltpu.VMEM((4, 4, 2, 2, 16, D), bf16), pltpu.VMEM((4, 4, 2, 16, D), bf16),
        pltpu.VMEM((4, 3, 2, 16, D), bf16), four, four, four,
        block, block, block, block,
        piece, piece, one, piece, one, piece, one, pltpu.VMEM((4, 16, HALF_D), bf16),
        pltpu.VMEM((512, K), bf16), pltpu.VMEM((512, K), bf16),
        image, pltpu.VMEM((64, 320), f32), weight, weight,
        pltpu.SemaphoreType.DMA((9,)),
        pltpu.SemaphoreType.DMA((N_SEMS,)),
        pltpu.SemaphoreType.DMA((N_SEMS,)),
    ]
    anywhere = pl.BlockSpec(memory_space=pl.ANY)
    shapes = (
        jax.ShapeDtypeStruct((128, D), bf16),
        jax.ShapeDtypeStruct((64, 320), f32),
        jax.ShapeDtypeStruct((D, K), bf16),
        jax.ShapeDtypeStruct((D, K), bf16),
    )
    made = pl.pallas_call(
        kernel,
        out_shape=shapes,
        in_specs=[anywhere] * 5,
        out_specs=(anywhere,) * 4,
        scratch_shapes=scratch,
        compiler_params=pltpu.CompilerParams(
            collective_id=0, has_side_effects=True, vmem_limit_bytes=56 * 2**20
        ),
        cost_estimate=pl.CostEstimate(flops=4 * 10**9, bytes_accessed=6 * 10**6, transcendentals=500000),
    )(tokens[0], grad_out[0], router.T, up_weight[0], down_weight[0])
    gx, gr, gu, gd = pl.pallas_call(
        keep,
        out_shape=shapes,
        in_specs=[anywhere] * 4,
        out_specs=(anywhere,) * 4,
        scratch_shapes=[
            image, pltpu.VMEM((64, 320), f32), weight, weight, pltpu.SemaphoreType.DMA((2, 4, 2))
        ],
        compiler_params=pltpu.CompilerParams(vmem_limit_bytes=56 * 2**20),
    )(*made)
    return (gx[None], gr.T, gu[None], gd[None])


def solution(mesh):
    placed = (
        P(("expert", "dp"), None, None),
        P(("expert", "dp"), None, None),
        P(),
        P("expert", None, "dp"),
        P("expert", None, "dp"),
    )
    return jax.shard_map(
        local,
        mesh=mesh,
        in_specs=placed,
        out_specs=(
            P(("expert", "dp"), None, None),
            P("dp", None),
            P("expert", None, "dp"),
            P("expert", None, "dp"),
        ),
        check_vma=False,
    )
```

time: 139 us -> 103 us (0.74)
  Pallas kernels: 132 us -> 102 us
  local copies, waits for them, and re-layouts: 5.67 us -> 0 us
    pallas_call x1 -> x2, Pallas kernels: 132 us -> 102 us  [the longest x1 99.1 us: local(): pl.pallas_call(kernel, out_shape=shapes, in_specs=[anywhere] * 5, out_spe...]
    unnamed x8 -> x0, local copies, waits for them, and re-layouts: 5.67 us -> none
where the time goes in v3:
time: 103 us; the launch traced here: 102 us
  Pallas kernels  102 us (99%)
    pallas_call x1, Pallas kernels, local(): pl.pallas_call(kernel, out_shape=shapes, in_specs=[anywhere] * 5, out_spe...  99.1 us
    pallas_call x1, Pallas kernels, local(): pl.pallas_call(keep, out_shape=shapes, in_specs=[anywhere] * 4, out_specs...  2.56 us

profile of v3, /device:TPU:1, one launch (start us, length us, event | category | flops | bytes accessed | tf_op | source)
XLA Modules:
  0.0 102.3 jit_solution(17509989344397900759)
XLA Ops:
  0.6 99.1 %shard_map.84 = (bf16[128,1280]{1,0:T(8,128)(2,1)}, f32[64,320]{1,0:T(8,128)}, bf16[1280,384]{1,0:T(8,128)(2,1)}, bf16[1280,384]{1,0:T(8,128)(2,1)}) custom-call(bf16[128,1280]{1,0:T(8,128)(2,1)} %bitcast.13, bf16[128,1280]{1,0:T(8,128)(2,1)} %bitcast.14, bf16[64,1280]{1,0:T(8,128)(2,1)} %bitcast.16, bf16[1280,384]{1,0:T(8,128)(2,1)} %bitcast.9, ...), custom_call_target="tpu_custom_call" | custom-call | flops 4000000000 | bytes 6000000 | tf_op jit(solution)/shard_map/pallas_call | solution.py:465
  99.7 2.6 %shard_map.85 = (bf16[128,1280]{1,0:T(8,128)(2,1)}, f32[64,320]{1,0:T(8,128)}, bf16[1280,384]{1,0:T(8,128)(2,1)}, bf16[1280,384]{1,0:T(8,128)(2,1)}) custom-call(bf16[128,1280]{1,0:T(8,128)(2,1)} %get-tuple-element.12.refs_0_, f32[64,320]{1,0:T(8,128)} %get-tuple-element.13.refs_1_, bf16[1280,384]{1,0:T(8,128)(2,1)} %get-tuple-element.14.refs_2_, ...), custom_call_target="tpu_custom_call" | custom-call | tf_op jit(solution)/shard_map/pallas_call | solution.py:476

commit v4 on v3

--- a/solution.py
+++ b/solution.py
@@ -15,6 +15,7 @@
 D = 1280
 K = 384
 HALF_D = 640
+ORDER = 'A3A2A1B3C3A0B2C2D3B1C1E3D2B0C0E2D1G3E1D0G2E0G1G0'
 
 
 def dot(a, b, ca, cb):
@@ -146,7 +147,7 @@
             [(x_hbm, x_ref), (rt_hbm, rt_ref), (go_hbm, go_ref), (wu_hbm, wu_ref), (wd_hbm, wd_ref)]
         )
     ]
-    for c in loads:
+    for c in loads[:3]:
         c.start()
 
     ex, dp = lax.axis_index("expert"), lax.axis_index("dp")
@@ -213,6 +214,7 @@
             c.start()
             pending.append((c, None))
         dst[slot] = src[...]
+        drain(n - 1)
         for d in range(1, n):
             came = (slot - d + n) % n
             copy(src, dst.at[came], at + d - 1, at + d - 1, partners[d - 1]).wait_recv()
@@ -237,6 +239,11 @@
 
     def cross_wait(at, n, dst, source):
         unless(keeps if n == SELF else None, copy(dst, dst, at + n, at + n, source[:2]).wait_recv)
+
+    def drain(keep):
+        while len(pending) > keep:
+            c, me = pending.pop(0)
+            unless(me, c.wait_send)
 
     def send(src, dst, to):
         at = sems_of(1)
@@ -247,6 +254,8 @@
 
     for c in loads[:3]:
         c.wait()
+    for c in loads[3:]:
+        c.start()
     x, go, rt = x_ref[...], go_ref[...], rt_ref[...]
     *saved, slots, grads = front(x, go, rt)
     slotted = jnp.concatenate([slots, grads], axis=0)
@@ -256,7 +265,7 @@
     all_to_all(s1, r1)()
     s2[...] = moved(swapped, r1[...].reshape(128, D)).reshape(N, 16, D)
     at2, at3 = sems_of(N), sems_of(N)
-    for j in range(N):
+    for j in (6, 7, 4, 5, 2, 3, 0, 1):
         g, t, i = outs[j]
         cross_send(at2, j, s2.at[j], xg.at[t, i], xg.at[M, SELF], outs[j])
 
@@ -273,21 +282,20 @@
     def spread(m, q, name, to):
         marks[name, q] = send(rows_of(m, q), rows_of(m, q), to)
 
+    O = (G, md)
+
     def stage_a(q):
         for i in (2 * q, 2 * q + 1):
             cross_wait(at2, i, xg.at[M, i], ins[i])
         spread(M, q, "y", Y)
         spread(M, q, "z", Z)
+        spread(M, q, "d", O)
         spread(M, q, "s", S)
 
     def stage_b(q):
         marks["y", q].wait_recv()
-        if q < 2:
-            spread(my, q, "d", Z)
         spread(my, q, "sy", S)
         marks["z", q].wait_recv()
-        if q >= 2:
-            spread(mz, q, "d", Y)
         spread(mz, q, "sz", S)
 
     def stage_c(q):
@@ -297,7 +305,7 @@
     def stage_d(q):
         for name in ("s", "sy", "sz", "sd"):
             marks[name, q].wait_recv()
-        if q == 0:
+        if str(q) == ORDER[ORDER.index("D") + 1]:
             loads[3].wait()
             loads[4].wait()
         wu, wd = wu_ref[...], wd_ref[...]
@@ -329,39 +337,28 @@
 
     def stage_e(q):
         marks["p", q].wait_recv()
-        diagonal = chip_sum(q, chip_d)
-        if q < 2:
-            forward(q, 0, diagonal, rel, "r", Z)
-            forward(q, 1, chip_sum(q, chip_z), fz, "fz", Z)
-        else:
-            forward(q, 0, diagonal, rel, "r", Y)
-            forward(q, 1, chip_sum(q, chip_y), fy, "fy", Y)
-
-    def stage_f(q):
-        marks["r", q].wait_recv()
-        if q < 2:
-            forward(q, 2, chip_sum(q, chip_y) + rel[q].astype(f32), fy, "fy", Y)
-        else:
-            forward(q, 2, chip_sum(q, chip_z) + rel[q].astype(f32), fz, "fz", Z)
+        forward(q, 0, chip_sum(q, chip_d), rel, "r", O)
+        forward(q, 1, chip_sum(q, chip_z), fz, "fz", Z)
+        forward(q, 2, chip_sum(q, chip_y), fy, "fy", Y)
 
     def stage_g(q):
-        marks["fy", q].wait_recv()
-        marks["fz", q].wait_recv()
-        total = chip_sum(q, chip) + fy[q].astype(f32) + fz[q].astype(f32)
+        for name in ("fy", "fz", "r"):
+            marks[name, q].wait_recv()
+        total = chip_sum(q, chip) + fy[q].astype(f32) + fz[q].astype(f32) + rel[q].astype(f32)
         s3[2 * q : 2 * q + 2] = total.astype(bf16)
-        for i in (2 * q, 2 * q + 1):
+        for i in (2 * q + 1, 2 * q):
             g, t, j = ins[i]
             cross_send(at3, i, s3.at[i], r3.at[j], r3.at[SELF], ins[i])
 
-    chain = ((stage_a, 0), (stage_b, 1), (stage_c, 2), (stage_e, 4), (stage_f, 5), (stage_g, 6), (stage_d, 3))
-    for t in range(4 + 6):
-        for run, late in chain:
-            if 0 <= t - late < 4:
-                run(t - late)
+    stages = {"A": stage_a, "B": stage_b, "C": stage_c, "D": stage_d, "E": stage_e, "G": stage_g}
+    for n in range(len(ORDER) // 2):
+        stages[ORDER[2 * n]](int(ORDER[2 * n + 1]))
 
     gd[...] = dot(gs[...], act_ref[...], 0, 0).astype(bf16)
     stores = [pltpu.make_async_copy(gd, gd_hbm, lsem.at[6])]
     stores[0].start()
+
+    drain(8)
 
     for j in range(N):
         cross_wait(at3, j, r3.at[j], outs[j])
@@ -370,6 +367,7 @@
     gu[...] = dot(xs[...], dpre_ref[...], 0, 0).astype(bf16)
     stores.append(pltpu.make_async_copy(gu, gu_hbm, lsem.at[5]))
     stores[1].start()
+    drain(7)
     wait()
     got = moved(by_expert(G), r4[...].reshape(128, D))
     slots_out, grad_slots = got[:64], got[64:]
@@ -402,8 +400,7 @@
     stores.append(pltpu.make_async_copy(gr, gr_hbm, lsem.at[8]))
     stores[3].start()
 
-    for c, me in pending:
-        unless(me, c.wait_send)
+    drain(0)
     for c in stores:
         c.wait()
 

time: 103 us -> 98.6 us (0.957)
  Pallas kernels: 102 us -> 97.5 us
    pallas_call x1, Pallas kernels: 99.1 us -> 94.9 us  [local(): pl.pallas_call(kernel, out_shape=shapes, in_specs=[anywhere] * 5, out_spe...]
where the time goes in v4:
time: 98.6 us; the launch traced here: 98.1 us
  Pallas kernels  97.5 us (99%)
    pallas_call x1, Pallas kernels, local(): pl.pallas_call(kernel, out_shape=shapes, in_specs=[anywhere] * 5, out_spe...  94.9 us
    pallas_call x1, Pallas kernels, local(): pl.pallas_call(keep, out_shape=shapes, in_specs=[anywhere] * 4, out_specs...  2.56 us

profile of v4, /device:TPU:1, one launch (start us, length us, event | category | flops | bytes accessed | tf_op | source)
XLA Modules:
  0.0 98.1 jit_solution(17261810455055443465)
XLA Ops:
  0.6 94.9 %shard_map.84 = (bf16[128,1280]{1,0:T(8,128)(2,1)}, f32[64,320]{1,0:T(8,128)}, bf16[1280,384]{1,0:T(8,128)(2,1)}, bf16[1280,384]{1,0:T(8,128)(2,1)}) custom-call(bf16[128,1280]{1,0:T(8,128)(2,1)} %bitcast.13, bf16[128,1280]{1,0:T(8,128)(2,1)} %bitcast.14, bf16[64,1280]{1,0:T(8,128)(2,1)} %bitcast.16, bf16[1280,384]{1,0:T(8,128)(2,1)} %bitcast.9, ...), custom_call_target="tpu_custom_call" | custom-call | flops 4000000000 | bytes 6000000 | tf_op jit(solution)/shard_map/pallas_call | solution.py:462
  95.6 2.6 %shard_map.85 = (bf16[128,1280]{1,0:T(8,128)(2,1)}, f32[64,320]{1,0:T(8,128)}, bf16[1280,384]{1,0:T(8,128)(2,1)}, bf16[1280,384]{1,0:T(8,128)(2,1)}) custom-call(bf16[128,1280]{1,0:T(8,128)(2,1)} %get-tuple-element.12.refs_0_, f32[64,320]{1,0:T(8,128)} %get-tuple-element.13.refs_1_, bf16[1280,384]{1,0:T(8,128)(2,1)} %get-tuple-element.14.refs_2_, ...), custom_call_target="tpu_custom_call" | custom-call | tf_op jit(solution)/shard_map/pallas_call | solution.py:473

commit v5 on v4

--- a/solution.py
+++ b/solution.py
@@ -90,8 +90,8 @@
     return (o & 7) * 16 + ((o >> 3) & 1) * 8 + (o >> 4)
 
 
-def moved(source, value, inverse=False):
-    return dot(pick(source, inverse), value, 1, 0).astype(bf16)
+def moved(one_hot, value):
+    return dot(one_hot, value, 1, 0).astype(bf16)
 
 
 def to_row(column):
@@ -138,7 +138,7 @@
     x_hbm, go_hbm, rt_hbm, wu_hbm, wd_hbm, gx_hbm, gr_hbm, gu_hbm, gd_hbm,
     x_ref, go_ref, rt_ref, wu_ref, wd_ref,
     s1, r1, s2, xg, xs, gs, parts, sibr, cs, rel, fy, fz, s3, r3, s4, r4,
-    tp, q1, t2, q2, t3, q3, t4, ro, act_ref, dpre_ref, gx, gr, gu, gd,
+    tp, q1, t2, q2, t3, q3, t4, ro, act_ref, dpre_ref, gx, gr, gu, gd, to_members, to_experts, swap,
     lsem, ssem, rsem,
 ):
     loads = [
@@ -168,10 +168,10 @@
     def greet(g, m):
         pl.semaphore_signal(barrier, inc=1, device_id=dev(g, m), device_id_type=MESH)
 
-    for g, m in group + far + near:
+    for g, m in group:
         greet(g, m)
     for n in range(N):
-        for g, m, _ in (outs[n], ins[n]):
+        for g, m, _ in (ins[n],):
             if n == SELF:
                 pl.when(jnp.logical_not(keeps))(functools.partial(greet, g, m))
             else:
@@ -252,6 +252,9 @@
         pending.append((c, None))
         return c
 
+    to_members[...] = pick(by_expert(G), inverse=True)
+    to_experts[...] = pick(by_expert(G))
+    swap[...] = pick(swapped)
     for c in loads[:3]:
         c.wait()
     for c in loads[3:]:
@@ -259,11 +262,11 @@
     x, go, rt = x_ref[...], go_ref[...], rt_ref[...]
     *saved, slots, grads = front(x, go, rt)
     slotted = jnp.concatenate([slots, grads], axis=0)
-    s1[...] = moved(by_expert(G), slotted, inverse=True).reshape(N, 16, D)
-    pl.semaphore_wait(barrier, 7 * 3 + 16 - 2 * (1 - jnp.minimum(M, 1)))
+    s1[...] = moved(to_members[...], slotted).reshape(N, 16, D)
+    pl.semaphore_wait(barrier, 7 + 8 - (1 - jnp.minimum(M, 1)))
 
     all_to_all(s1, r1)()
-    s2[...] = moved(swapped, r1[...].reshape(128, D)).reshape(N, 16, D)
+    s2[...] = moved(swap[...], r1[...].reshape(128, D)).reshape(N, 16, D)
     at2, at3 = sems_of(N), sems_of(N)
     for j in (6, 7, 4, 5, 2, 3, 0, 1):
         g, t, i = outs[j]
@@ -287,10 +290,10 @@
     def stage_a(q):
         for i in (2 * q, 2 * q + 1):
             cross_wait(at2, i, xg.at[M, i], ins[i])
+        spread(M, q, "s", S)
+        spread(M, q, "d", O)
         spread(M, q, "y", Y)
         spread(M, q, "z", Z)
-        spread(M, q, "d", O)
-        spread(M, q, "s", S)
 
     def stage_b(q):
         marks["y", q].wait_recv()
@@ -362,14 +365,14 @@
 
     for j in range(N):
         cross_wait(at3, j, r3.at[j], outs[j])
-    s4[...] = moved(swapped, r3[...].reshape(128, D)).reshape(N, 16, D)
+    s4[...] = moved(swap[...], r3[...].reshape(128, D)).reshape(N, 16, D)
     wait = all_to_all(s4, r4)
     gu[...] = dot(xs[...], dpre_ref[...], 0, 0).astype(bf16)
     stores.append(pltpu.make_async_copy(gu, gu_hbm, lsem.at[5]))
     stores[1].start()
     drain(7)
     wait()
-    got = moved(by_expert(G), r4[...].reshape(128, D))
+    got = moved(to_experts[...], r4[...].reshape(128, D))
     slots_out, grad_slots = got[:64], got[64:]
     x, go, rt = x_ref[...], go_ref[...], rt_ref[...]
     hi, lo, row, term = back(x, go, rt, saved, slots_out, grad_slots)
@@ -438,6 +441,7 @@
     weight = pltpu.VMEM((D, K), bf16)
     image = pltpu.VMEM((128, D), bf16)
     four = pltpu.VMEM((4, 2, 16, D), bf16)
+    moves = pltpu.VMEM((128, 128), bf16)
     scratch = [
         image, image, pltpu.VMEM((64, D), bf16), weight, weight,
         block, block, block, pltpu.VMEM((N, N, 16, D), bf16),
@@ -447,7 +451,7 @@
         block, block, block, block,
         piece, piece, one, piece, one, piece, one, pltpu.VMEM((4, 16, HALF_D), bf16),
         pltpu.VMEM((512, K), bf16), pltpu.VMEM((512, K), bf16),
-        image, pltpu.VMEM((64, 320), f32), weight, weight,
+        image, pltpu.VMEM((64, 320), f32), weight, weight, moves, moves, moves,
         pltpu.SemaphoreType.DMA((9,)),
         pltpu.SemaphoreType.DMA((N_SEMS,)),
         pltpu.SemaphoreType.DMA((N_SEMS,)),

time: 98.6 us -> 98 us (level)
  no operation moved by 1% of the time
where the time goes in v5:
time: 98 us; the launch traced here: 97.5 us
  Pallas kernels  96.9 us (99%)
    pallas_call x1, Pallas kernels, local(): pl.pallas_call(kernel, out_shape=shapes, in_specs=[anywhere] * 5, out_spe...  94.3 us
    pallas_call x1, Pallas kernels, local(): pl.pallas_call(keep, out_shape=shapes, in_specs=[anywhere] * 4, out_specs...  2.56 us

profile of v5, /device:TPU:1, one launch (start us, length us, event | category | flops | bytes accessed | tf_op | source)
XLA Modules:
  0.0 97.5 jit_solution(8710538283629920155)
XLA Ops:
  0.6 94.3 %shard_map.84 = (bf16[128,1280]{1,0:T(8,128)(2,1)}, f32[64,320]{1,0:T(8,128)}, bf16[1280,384]{1,0:T(8,128)(2,1)}, bf16[1280,384]{1,0:T(8,128)(2,1)}) custom-call(bf16[128,1280]{1,0:T(8,128)(2,1)} %bitcast.13, bf16[128,1280]{1,0:T(8,128)(2,1)} %bitcast.14, bf16[64,1280]{1,0:T(8,128)(2,1)} %bitcast.16, bf16[1280,384]{1,0:T(8,128)(2,1)} %bitcast.9, ...), custom_call_target="tpu_custom_call" | custom-call | flops 4000000000 | bytes 6000000 | tf_op jit(solution)/shard_map/pallas_call | solution.py:466
  95.0 2.6 %shard_map.85 = (bf16[128,1280]{1,0:T(8,128)(2,1)}, f32[64,320]{1,0:T(8,128)}, bf16[1280,384]{1,0:T(8,128)(2,1)}, bf16[1280,384]{1,0:T(8,128)(2,1)}) custom-call(bf16[128,1280]{1,0:T(8,128)(2,1)} %get-tuple-element.12.refs_0_, f32[64,320]{1,0:T(8,128)} %get-tuple-element.13.refs_1_, bf16[1280,384]{1,0:T(8,128)(2,1)} %get-tuple-element.14.refs_2_, ...), custom_call_target="tpu_custom_call" | custom-call | tf_op jit(solution)/shard_map/pallas_call | solution.py:477

commit v6 on v5

--- a/solution.py
+++ b/solution.py
@@ -329,7 +329,8 @@
         back_out = dot(dpre, wu, 1, 1).reshape(16, 1, 8, D)
         mixed = jnp.concatenate([out, back_out], axis=1).reshape(16, 16, D).astype(bf16)
         parts[q] = mixed.reshape(4, 2, 2, 16, D)
-        marks["p", q] = send(parts.at[q, :, 1 - c0], sibr.at[q], S)
+        for name, to in (("pd", chip_d), ("pz", chip_z), ("py", chip_y), ("p", chip)):
+            marks[name, q] = send(parts.at[q, to, 1 - c0], sibr.at[q, to], S)
 
     def chip_sum(q, to):
         return parts[q, to, c0].astype(f32) + sibr[q, to].astype(f32)
@@ -339,13 +340,15 @@
         marks[name, q] = send(cs.at[q, n], dst.at[q], to)
 
     def stage_e(q):
-        marks["p", q].wait_recv()
+        marks["pd", q].wait_recv()
         forward(q, 0, chip_sum(q, chip_d), rel, "r", O)
+        marks["pz", q].wait_recv()
         forward(q, 1, chip_sum(q, chip_z), fz, "fz", Z)
+        marks["py", q].wait_recv()
         forward(q, 2, chip_sum(q, chip_y), fy, "fy", Y)
 
     def stage_g(q):
-        for name in ("fy", "fz", "r"):
+        for name in ("p", "fy", "fz", "r"):
             marks[name, q].wait_recv()
         total = chip_sum(q, chip) + fy[q].astype(f32) + fz[q].astype(f32) + rel[q].astype(f32)
         s3[2 * q : 2 * q + 2] = total.astype(bf16)
@@ -431,7 +434,7 @@
         two.wait()
 
 
-N_SEMS = 7 + 8 + 8 + 4 * (7 + 4) + 7 + 7 + 7 + 7 + 3
+N_SEMS = 7 + 8 + 8 + 4 * (7 + 7) + 7 + 7 + 7 + 7 + 3
 
 
 def local(tokens, grad_out, router, up_weight, down_weight):

time: 98 us -> 98.8 us (level)
  Pallas kernels: 96.9 us -> 98 us
    pallas_call x1, Pallas kernels: 94.3 us -> 95.4 us  [local(): pl.pallas_call(kernel, out_shape=shapes, in_specs=[anywhere] * 5, out_spe...]
where the time goes in v6:
time: 98.8 us; the launch traced here: 98.6 us
  Pallas kernels  98 us (99%)
    pallas_call x1, Pallas kernels, local(): pl.pallas_call(kernel, out_shape=shapes, in_specs=[anywhere] * 5, out_spe...  95.4 us
    pallas_call x1, Pallas kernels, local(): pl.pallas_call(keep, out_shape=shapes, in_specs=[anywhere] * 4, out_specs...  2.56 us

profile of v6, /device:TPU:1, one launch (start us, length us, event | category | flops | bytes accessed | tf_op | source)
XLA Modules:
  0.0 98.6 jit_solution(1449611945455166487)
XLA Ops:
  0.6 95.4 %shard_map.84 = (bf16[128,1280]{1,0:T(8,128)(2,1)}, f32[64,320]{1,0:T(8,128)}, bf16[1280,384]{1,0:T(8,128)(2,1)}, bf16[1280,384]{1,0:T(8,128)(2,1)}) custom-call(bf16[128,1280]{1,0:T(8,128)(2,1)} %bitcast.13, bf16[128,1280]{1,0:T(8,128)(2,1)} %bitcast.14, bf16[64,1280]{1,0:T(8,128)(2,1)} %bitcast.16, bf16[1280,384]{1,0:T(8,128)(2,1)} %bitcast.9, ...), custom_call_target="tpu_custom_call" | custom-call | flops 4000000000 | bytes 6000000 | tf_op jit(solution)/shard_map/pallas_call | solution.py:469
  96.0 2.6 %shard_map.85 = (bf16[128,1280]{1,0:T(8,128)(2,1)}, f32[64,320]{1,0:T(8,128)}, bf16[1280,384]{1,0:T(8,128)(2,1)}, bf16[1280,384]{1,0:T(8,128)(2,1)}) custom-call(bf16[128,1280]{1,0:T(8,128)(2,1)} %get-tuple-element.12.refs_0_, f32[64,320]{1,0:T(8,128)} %get-tuple-element.13.refs_1_, bf16[1280,384]{1,0:T(8,128)(2,1)} %get-tuple-element.14.refs_2_, ...), custom_call_target="tpu_custom_call" | custom-call | tf_op jit(solution)/shard_map/pallas_call | solution.py:480
